TPU v7x, 256 devices: a whole 4x4x8 slice. The times are simulated.
256 devices in a mesh: blk: 8 (over x_hi, y), grp: 32 (over x_lo, z, core).
Axes of the slice: x: 4 (x_hi: 2, x_lo: 2; x = x_hi * 2 + x_lo), y: 4, z: 8, core: 2. Of those that a mesh axis runs over, the one named last changes fastest.
Arguments:
- spot_features: bfloat16 [64, 49152], P(None, ('blk', 'grp')), may hold values from -32 to 32
- spot_factors: bfloat16 [34, 49152], P(None, ('blk', 'grp')), may hold values from -52 to 52
- spot_log_mass: float32 [49152], P(('blk', 'grp')), may hold values from -1 to 1
- cell_features: bfloat16 [64, 49152], P(None, ('blk', 'grp')), may hold values from -2 to 2
- cell_factors: bfloat16 [34, 49152], P(None, ('blk', 'grp')), may hold values from -1 to 1
- cell_log_mass: float32 [49152], P(('blk', 'grp')), may hold values from -1 to 1
- cell_potential: float32 [49152], P(('blk', 'grp')), may hold values from -50 to 1
Outputs:
- spot_potential: float32 [49152], P(('blk', 'grp'))
- cell_update: float32 [49152], P(('blk', 'grp'))
All inputs are finite; a program needn't handle non-finite values.
Results may differ from a plain program's by a relative error of at most 0.0003.
Values may be sent and summed in bfloat16 or wider, within the bound.
A program may use at most 128 MiB of HBM per device.

v0:
```python
import math

import jax
import jax.numpy as jnp
from jax import lax
from jax.sharding import PartitionSpec as P

epsilon = 0.25
tile_budget = 2097152


def joined(value, axis, join):
    pieces = jax.tree.map(lambda part: lax.all_gather(part, axis), value)
    head = jax.tree.map(lambda part: part[0], pieces)
    tail = jax.tree.map(lambda part: part[1:], pieces)
    so_far, _ = lax.scan(lambda so_far, section: (join(so_far, section), None), head, tail)
    return so_far


def squares(features):
    values = features.astype(jnp.float32)
    return jnp.sum(values * values, axis=0)


def contract(left_side, right_side):
    return lax.dot_general(
        left_side, right_side, (((0,), (0,)), ((), ())), preferred_element_type=jnp.float32
    )


def absorb(state_pair, scores):
    running, exp_total = state_pair
    newest = jnp.maximum(running, jnp.max(scores, axis=1))
    exp_total = exp_total * jnp.exp(running - newest) + jnp.sum(
        jnp.exp(scores - newest[:, None]), axis=1
    )
    return (newest, exp_total)


def combine(earlier, second):
    newest = jnp.maximum(earlier[0], second[0])
    return (
        newest,
        earlier[1] * jnp.exp(earlier[0] - newest) + second[1] * jnp.exp(second[0] - newest),
    )


def fold_columns(state_pair, row_feat, row_fac, row_term, col_feat, col_fac, col_offset):
    col_width = col_feat.shape[1]
    row_count = row_feat.shape[1]
    col_block = col_width
    while col_block * row_count > tile_budget and col_block % 2 == 0:
        col_block = col_block // 2
    cross_scale = 2.0 / row_feat.shape[0]

    def tile_step(position, inner_pair):
        first_col = position * col_block
        piece_feat = lax.dynamic_slice_in_dim(col_feat, first_col, col_block, 1)
        piece_fac = lax.dynamic_slice_in_dim(col_fac, first_col, col_block, 1)
        piece_offset = lax.dynamic_slice_in_dim(col_offset, first_col, col_block, 0)
        scores = (
            row_term[:, None]
            + piece_offset[None, :]
            + (cross_scale * contract(row_feat, piece_feat) - contract(row_fac, piece_fac))
            / epsilon
        )
        return absorb(inner_pair, scores)

    col_count = col_width // col_block
    return lax.fori_loop(0, col_count, tile_step, state_pair)


def settle(running, exp_total, row_mass, col_total):
    return epsilon * (row_mass - (running + jnp.log(exp_total) - math.log(col_total)))


def own_offsets(col_feat, col_pot):
    return (col_pot - squares(col_feat) / col_feat.shape[0]) / epsilon


def every_offset(col_feat, col_pot):
    return lax.all_gather(own_offsets(col_feat, col_pot), ("blk", "grp"), axis=0, tiled=True)


def empty_pair(row_count):
    return (jnp.full((row_count,), -jnp.inf, jnp.float32), jnp.zeros((row_count,), jnp.float32))


def split_half(row_feat, row_fac, row_mass, col_feat, col_fac, col_pot):
    group_size = lax.axis_size("grp")
    loop_size = lax.axis_size("blk")
    local_count = col_feat.shape[1]
    rows_feat, rows_fac = (
        lax.all_gather(row_feat, "grp", axis=1, tiled=True),
        lax.all_gather(row_fac, "grp", axis=1, tiled=True),
    )
    all_offset = every_offset(col_feat, col_pot)
    offset_table = all_offset.reshape(loop_size, group_size, local_count)
    my_offsets = lax.dynamic_index_in_dim(
        offset_table, lax.axis_index("grp"), 1, keepdims=False
    ).reshape(loop_size * local_count)
    row_term = -squares(rows_feat) / (rows_feat.shape[0] * epsilon)
    piece_feat = lax.all_gather(col_feat, "blk", axis=1, tiled=True)
    piece_fac = lax.all_gather(col_fac, "blk", axis=1, tiled=True)
    running, exp_total = fold_columns(
        empty_pair(rows_feat.shape[1]),
        rows_feat,
        rows_fac,
        row_term,
        piece_feat,
        piece_fac,
        my_offsets,
    )
    running, exp_total = joined((running, exp_total), "grp", combine)
    own_count = row_feat.shape[1]
    first_row = lax.axis_index("grp") * own_count
    running = lax.dynamic_slice_in_dim(running, first_row, own_count, 0)
    exp_total = lax.dynamic_slice_in_dim(exp_total, first_row, own_count, 0)
    return settle(running, exp_total, row_mass, local_count * loop_size * group_size)


def local(
    spot_features,
    spot_factors,
    spot_log_mass,
    cell_features,
    cell_factors,
    cell_log_mass,
    cell_potential,
):
    spot_potential = split_half(
        spot_features, spot_factors, spot_log_mass, cell_features, cell_factors, cell_potential
    )
    cell_update = split_half(
        cell_features, cell_factors, cell_log_mass, spot_features, spot_factors, spot_potential
    )
    return (spot_potential, cell_update)


def solution(mesh):
    placed = (
        P(None, ("blk", "grp")),
        P(None, ("blk", "grp")),
        P(("blk", "grp")),
        P(None, ("blk", "grp")),
        P(None, ("blk", "grp")),
        P(("blk", "grp")),
        P(("blk", "grp")),
    )
    return jax.shard_map(
        local,
        mesh=mesh,
        in_specs=placed,
        out_specs=(P(("blk", "grp")), P(("blk", "grp"))),
        check_vma=False,
    )
```

profile of v0, /device:TPU:1, one launch (start us, length us, event | category | flops | bytes accessed | tf_op | source)
XLA Modules:
  0.0 864.2 jit_solution(13601665995321360344)
XLA Ops:
  9.7 31.7 %all-gather.5 = bf16[8,192,64]{1,2,0:T(8,128)(2,1)} all-gather(bf16[1,192,64]{1,2,0:T(8,128)(2,1)} %bitcast.82), channel_id=1, replica_groups=mesh['blk'=8,'grp'=32] {'blk'}, dimensions={0}, use_global_device_ids=true | all-gather | bytes 221184 | tf_op jit(solution)/shard_map/all_gather | solution.py:103
  41.4 49.3 %all-gather.8 = bf16[32,192,64]{1,2,0:T(8,128)(2,1)} all-gather(bf16[1,192,64]{1,2,0:T(8,128)(2,1)} %bitcast.83), channel_id=1, replica_groups=mesh['blk'=8,'grp'=32] {'grp'}, dimensions={0}, use_global_device_ids=true | all-gather | bytes 811008 | tf_op jit(solution)/shard_map/all_gather | solution.py:94
  90.7 30.4 %all-gather.6 = bf16[8,192,34]{1,2,0:T(8,128)(2,1)} all-gather(bf16[1,192,34]{1,2,0:T(8,128)(2,1)} %bitcast.86), channel_id=1, replica_groups=mesh['blk'=8,'grp'=32] {'blk'}, dimensions={0}, use_global_device_ids=true | all-gather | bytes 117504 | tf_op jit(solution)/shard_map/all_gather | solution.py:104
  121.1 38.5 %all-gather.11 = bf16[32,192,34]{1,2,0:T(8,128)(2,1)S(1)} all-gather(bf16[1,192,34]{1,2,0:T(8,128)(2,1)} %bitcast.87), channel_id=1, replica_groups=mesh['blk'=8,'grp'=32] {'grp'}, dimensions={0}, use_global_device_ids=true | all-gather | bytes 430848 | tf_op jit(solution)/shard_map/all_gather | solution.py:95
  159.6 35.3 %all-gather.4 = bf16[32,192,64]{1,2,0:T(8,128)(2,1)S(1)} all-gather(bf16[1,192,64]{1,2,0:T(8,128)(2,1)} %bitcast.84), channel_id=1, replica_groups=mesh['blk'=8,'grp'=32] {'grp'}, dimensions={0}, use_global_device_ids=true | all-gather | bytes 811008 | tf_op jit(solution)/shard_map/all_gather | solution.py:94
  196.9 32.5 %all-gather.7 = bf16[32,192,34]{1,2,0:T(8,128)(2,1)S(1)} all-gather(bf16[1,192,34]{1,2,0:T(8,128)(2,1)S(1)} %bitcast.88), channel_id=1, replica_groups=mesh['blk'=8,'grp'=32] {'grp'}, dimensions={0}, use_global_device_ids=true | all-gather | bytes 430848 | tf_op jit(solution)/shard_map/all_gather | solution.py:95
  242.6 24.3 %all-reduce.7.cloned.1.call-done = f32[8,32,192]{2,1,0:T(8,128)} async-done(((f32[8,32,192]{2,1,0:T(8,128)}), f32[8,32,192]{2,1,0:T(8,128)}) %all-reduce.7.cloned.1.call-update) | async-done | bytes 196624
  267.8 73.5 %while.58 = (s32[]{:T(128)}, f32[6144]{0:T(1024)S(1)}, f32[6144]{0:T(1024)S(1)}, f32[6144]{0:T(1024)S(1)}, f32[1536]{0:T(1024)S(1)}, /*index=5*/bf16[64,1536]{1,...) while((s32[]{:T(128)}, f32[6144]{0:T(1024)S(1)}, ...), condition=%wide.region_5.6_spmd.clone, body=%wide.region_2.5_spmd.clone.sunk | while | flops 240678912 | bytes 20478400 | solution.py:70
  269.6 4.4 fusion.35
  274.0 3.0 exponential_reduce_fusion.4
  278.8 4.4 fusion.35
  283.1 3.0 exponential_reduce_fusion.4
  288.0 4.4 fusion.35
  292.3 3.0 exponential_reduce_fusion.4
  297.2 4.4 fusion.35
  301.5 3.0 exponential_reduce_fusion.4
  306.4 4.4 fusion.35
  310.7 3.0 exponential_reduce_fusion.4
  315.6 4.4 fusion.35
  324.8 4.4 fusion.35
  329.1 3.0 exponential_reduce_fusion.4
  333.9 4.3 fusion.35
  341.3 35.9 %all-gather = f32[196608]{0:T(1024)S(1)} all-gather(f32[6144]{0:T(1024)S(1)} %get-tuple-element.368), channel_id=2, replica_groups=mesh['blk'=8,'grp'=32] {'grp'}, dimensions={0}, use_global_device_ids=true | all-gather | bytes 811008 | tf_op jit(solution)/shard_map/all_gather | solution.py:13
  377.3 33.1 %all-gather.1 = f32[196608]{0:T(1024)S(1)} all-gather(f32[6144]{0:T(1024)S(1)} %get-tuple-element.369), channel_id=3, replica_groups=mesh['blk'=8,'grp'=32] {'grp'}, dimensions={0}, use_global_device_ids=true | all-gather | bytes 811008 | tf_op jit(solution)/shard_map/all_gather | solution.py:13
  412.4 34.5 %while.56 = (s32[]{:T(128)}, f32[6144]{0:T(1024)S(1)}, f32[6144]{0:T(1024)S(1)}, f32[31,6144]{1,0:T(8,128)}, f32[31,6144]{1,0:T(8,128)}, /*index=5*/s32[]{:T(128)}) while((s32[]{:T(128)}, f32[6144]{0:T(1024)S(1)}, f32[6144]{0:T(1024)S(1)}, f32[31,6144]{1,0:T(8,128)}, f32[31,6144]{1,0:T(8,128)}, /*index=5*/s32[]{:T(128)}) %tuple.111), condition=%wide.region_7.8_spmd, body=%wide.region_6.7_spmd.sunk | while | flops 36866 | bytes 245833 | solution.py:16
  448.5 28.5 %all-gather.9 = bf16[8,192,64]{1,2,0:T(8,128)(2,1)S(1)} all-gather(bf16[1,192,64]{1,2,0:T(8,128)(2,1)S(1)} %bitcast.85), channel_id=1, replica_groups=mesh['blk'=8,'grp'=32] {'blk'}, dimensions={0}, use_global_device_ids=true | all-gather | bytes 221184 | tf_op jit(solution)/shard_map/all_gather | solution.py:103
  477.3 28.2 %all-gather.10 = bf16[8,192,34]{1,2,0:T(8,128)(2,1)S(1)} all-gather(bf16[1,192,34]{1,2,0:T(8,128)(2,1)S(1)} %bitcast.89), channel_id=1, replica_groups=mesh['blk'=8,'grp'=32] {'blk'}, dimensions={0}, use_global_device_ids=true | all-gather | bytes 117504 | tf_op jit(solution)/shard_map/all_gather | solution.py:104
  505.7 187.9 %all-reduce.9.cloned.1.call-done = f32[8,32,192]{2,1,0:T(8,128)} async-done(((f32[8,32,192]{2,1,0:T(8,128)}), f32[8,32,192]{2,1,0:T(8,128)}) %all-reduce.9.cloned.1.call-update) | async-done | bytes 196624
  694.6 60.5 %while.59 = (s32[]{:T(128)}, f32[6144]{0:T(1024)S(1)}, f32[6144]{0:T(1024)S(1)}, f32[6144]{0:T(1024)S(1)}, f32[1536]{0:T(1024)S(1)}, /*index=5*/bf16[64,1536]{1,...) while((s32[]{:T(128)}, f32[6144]{0:T(1024)S(1)}, ...), condition=%wide.region_13.14_spmd.clone, body=%wide.region_10.13_spmd.clone.sunk | while | flops 240678912 | bytes 20552384 | solution.py:70
  695.5 3.5 fusion.40
  699.1 3.0 exponential_reduce_fusion.5
  703.1 3.5 fusion.40
  706.6 3.0 exponential_reduce_fusion.5
  710.7 3.5 fusion.40
  714.2 3.0 exponential_reduce_fusion.5
  718.2 3.5 fusion.40
  721.8 3.0 exponential_reduce_fusion.5
  725.8 3.5 fusion.40
  729.3 3.0 exponential_reduce_fusion.5
  733.4 3.5 fusion.40
  736.9 3.0 exponential_reduce_fusion.5
  740.9 3.5 fusion.40
  744.5 3.0 exponential_reduce_fusion.5
  748.5 3.5 fusion.40
  752.0 3.0 exponential_reduce_fusion.5
  755.1 35.9 %all-gather.2 = f32[196608]{0:T(1024)S(1)} all-gather(f32[6144]{0:T(1024)S(1)} %get-tuple-element.372), channel_id=4, replica_groups=mesh['blk'=8,'grp'=32] {'grp'}, dimensions={0}, use_global_device_ids=true | all-gather | bytes 811008 | tf_op jit(solution)/shard_map/all_gather | solution.py:13
  791.0 32.9 %all-gather.3 = f32[196608]{0:T(1024)S(1)} all-gather(f32[6144]{0:T(1024)S(1)} %get-tuple-element.373), channel_id=5, replica_groups=mesh['blk'=8,'grp'=32] {'grp'}, dimensions={0}, use_global_device_ids=true | all-gather | bytes 811008 | tf_op jit(solution)/shard_map/all_gather | solution.py:13
  825.1 31.6 %while.57 = (s32[]{:T(128)}, f32[6144]{0:T(1024)S(1)}, f32[6144]{0:T(1024)S(1)}, f32[31,6144]{1,0:T(8,128)S(1)}, f32[31,6144]{1,0:T(8,128)}, /*index=5*/s32[]{:T(128)}) while((s32[]{:T(128)}, f32[6144]{0:T(1024)S(1)}, f32[6144]{0:T(1024)S(1)}, f32[31,6144]{1,0:T(8,128)S(1)}, f32[31,6144]{1,0:T(8,128)}, /*index=5*/s32[]{:T(128)}) %tuple.117), condition=%wide.region_15.16_spmd, body=%wide.region_14.15_spmd.sunk | while | flops 36866 | bytes 245833 | solution.py:16
  (267 shorter events, 118.4 us)
Async XLA Ops:
  7.2 189.7 %copy-start.1 = (bf16[34,192]{1,0:T(8,128)(2,1)S(1)}, bf16[34,192]{1,0:T(8,128)(2,1)}, u32[]{:S(2)}) copy-start(bf16[34,192]{1,0:T(8,128)(2,1)} %param.16) | copy-start | bytes 39172
  7.2 259.7 %all-reduce.7.cloned.1.call-start = ((), (), s32[]{:S(2)}) async-start(), calls=%async_computation | async-start | bytes 524288
  9.7 683.9 %all-reduce.9.cloned.1.call-start = ((), (), s32[]{:S(2)}) async-start(), calls=%async_computation.1 | async-start | bytes 524288
  341.3 105.6 %copy-start.2 = (f32[192]{0:T(256)S(1)}, f32[192]{0:T(256)}, u32[]{:S(2)}) copy-start(f32[192]{0:T(256)} %param.17) | copy-start | bytes 2308
  377.2 71.3 %copy-start = (bf16[64,192]{1,0:T(8,128)(2,1)S(1)}, bf16[64,192]{1,0:T(8,128)(2,1)}, u32[]{:S(2)}) copy-start(bf16[64,192]{1,0:T(8,128)(2,1)} %param.15) | copy-start | bytes 73732
  755.1 101.6 %copy-start.3 = (f32[192]{0:T(256)S(1)}, f32[192]{0:T(256)}, u32[]{:S(2)}) copy-start(f32[192]{0:T(256)} %param.20) | copy-start | bytes 2308
Sparse Core Ops, SparseCore 0:
  13.5 253.3 all-reduce.6
  448.6 244.9 all-reduce.8
where the time goes:
time: 868 us; the launch traced here: 864 us
  blocking collectives  412 us (47%)
  waiting for transfers between devices  212 us (24%)
  local copies, waits for them, and re-layouts  85.6 us (10%)
  matrix products  83.4 us (10%)
  other arithmetic  54.5 us (6%)
  between operations  14.3 us (2%)
    unnamed x4, waiting for transfers between devices  212 us
    all_gather x4, blocking collectives, joined(): pieces = jax.tree.map(lambda part: lax.all_gather(part, axis), value)  138 us
    all_gather x2, blocking collectives, split_half(): lax.all_gather(row_feat, 'grp', axis=1, tiled=True)  84.6 us
    dot_general x32, matrix products, contract(): lax.dot_general(left_side, right_side, (((0,), (0,)), ((), ())), preferre...  83.4 us
    all_gather x2, blocking collectives, split_half(): lax.all_gather(row_fac, 'grp', axis=1, tiled=True)  71 us
    dynamic_slice x62, local copies, waits for them, and re-layouts, joined(): lax.scan(lambda so_far, section: (join(so_far, section), None), head, tail)  62.9 us
    all_gather x2, blocking collectives, split_half(): piece_feat = lax.all_gather(col_feat, 'blk', axis=1, tiled=True)  60.2 us
    all_gather x2, blocking collectives, split_half(): piece_fac = lax.all_gather(col_fac, 'blk', axis=1, tiled=True)  58.7 us
  transfers between devices with their start and end apart: 2, of which 2 were waited for; matrix products, arithmetic and copies ran while one was open for 2% of the time, Pallas kernels for 0%

commit v1 on v0

v1 whole, which is shorter than its diff:
```python
import math

import jax
import jax.numpy as jnp
from jax import lax
from jax.experimental import pallas as pl
from jax.experimental.pallas import tpu as pltpu
from jax.sharding import PartitionSpec as P

epsilon = 0.25
width = 192
depth = 128
features, factors = 64, 34
offset_lane = features + factors
dual_lane = offset_lane + 3
group = 16
rows = 768
lanes = 384
chunks = group * width // lanes
tiles = group * width // rows
lowest = -1e30
MESH = pl.DeviceIdType.MESH


def dot_first(left, right):
    return lax.dot_general(
        left, right, (((0,), (0,)), ((), ())), preferred_element_type=jnp.float32
    )


def dot_last(left, right):
    return lax.dot_general(
        left, right, (((1,), (1,)), ((), ())), preferred_element_type=jnp.float32
    )


def placing(count, first_lane, scale):
    source = lax.broadcasted_iota(jnp.int32, (count, depth), 0)
    lane = lax.broadcasted_iota(jnp.int32, (count, depth), 1)
    return jnp.where(lane == source + first_lane, scale, 0.0).astype(jnp.bfloat16)


def pieces(row):
    high = row.astype(jnp.bfloat16).astype(jnp.float32)
    rest = row - high
    middle = rest.astype(jnp.bfloat16).astype(jnp.float32)
    low = rest - middle
    at = lax.broadcasted_iota(jnp.int32, (16, row.shape[1]), 0)
    stacked = jnp.where(at == 0, high, jnp.where(at == 1, middle, jnp.where(at == 2, low, 0.0)))
    return stacked.astype(jnp.bfloat16)


def lane_between(first, last):
    lane = lax.broadcasted_iota(jnp.int32, (width, depth), 1)
    return (lane >= first) & (lane < last)


def norms(feat):
    values = feat.astype(jnp.float32)
    return jnp.sum(values * values, axis=0, keepdims=True) * (1.0 / (features * epsilon))


def z_shift(pair):
    return jnp.where(pair % 2 == 1, (pair + 1) // 2, (8 - pair // 2) % 8)


def z_shift_of(pair):
    return (pair + 1) // 2 if pair % 2 else (8 - pair // 2) % 8


def kernel(
    spot_feat, spot_fac, spot_mass, cell_feat, cell_fac, cell_mass, cell_pot,
    spot_out, cell_out,
    spots, cells, tile_a, tile_b, highest, total,
    part_1, out_1, dual, part_2, out_2,
    spot_send, spot_recv, cell_send, cell_recv,
    part_1_send, part_1_recv, dual_send, dual_recv, part_2_send, part_2_recv,
):
    blk, grp = lax.axis_index("blk"), lax.axis_index("grp")
    my_x, my_y = (blk // 4) * 2 + grp // 16, blk % 4
    my_z, my_core = (grp % 16) // 2, grp % 2

    def place(x, y, z, core):
        return ((x // 2) * 4 + y, (x % 2) * 16 + z * 2 + core)

    def along_q(shift, other):
        return place(my_x, my_y, (my_z + shift) % 8, (my_core + other) % 2)

    def along_p(dx, dy):
        return place((my_x + dx) % 4, (my_y + dy) % 4, my_z, my_core)

    barrier = pltpu.get_barrier_semaphore()
    for slot in range(1, group):
        pl.semaphore_signal(
            barrier, inc=1, device_id=along_q(z_shift_of(slot // 2), slot % 2), device_id_type=MESH
        )
        pl.semaphore_signal(
            barrier, inc=1, device_id=along_p(slot // 4, slot % 4), device_id_type=MESH
        )

    own_spots = (
        dot_first(spot_feat[...], placing(features, 0, 0.125))
        + dot_first(spot_fac[...], placing(factors, features, -4.0))
    )
    own_spots = jnp.where(lane_between(offset_lane, offset_lane + 3), 1.0, own_spots)
    spots[0:width, :] = own_spots.astype(jnp.bfloat16)
    cell_norm = norms(cell_feat[...])
    potential = cell_pot[...].reshape(1, width) * (1.0 / epsilon)
    own_cells = (
        dot_first(cell_feat[...], placing(features, 0, 1.0))
        + dot_first(cell_fac[...], placing(factors, features, 1.0))
        + dot_first(pieces(potential - cell_norm), placing(16, offset_lane, 1.0))
    )
    own_cells = jnp.where(lane_between(dual_lane, dual_lane + 3), 1.0, own_cells)
    cells[0:width, :] = own_cells.astype(jnp.bfloat16)

    pl.semaphore_wait(barrier, 2 * (group - 1))

    def spot_copy(slot):
        return pltpu.make_async_remote_copy(
            src_ref=spots.at[pl.ds(0, width), :],
            dst_ref=spots.at[pl.ds(slot * width, width), :],
            send_sem=spot_send.at[slot],
            recv_sem=spot_recv.at[slot],
            device_id=along_q(z_shift_of(slot // 2), slot % 2),
            device_id_type=MESH,
        )

    def cell_copy(slot):
        return pltpu.make_async_remote_copy(
            src_ref=cells.at[pl.ds(0, width), :],
            dst_ref=cells.at[pl.ds(slot * width, width), :],
            send_sem=cell_send.at[slot],
            recv_sem=cell_recv.at[slot],
            device_id=along_p(slot // 4, slot % 4),
            device_id_type=MESH,
        )

    near_first = (1, 3, 4, 12, 5, 7, 13, 15, 2, 8, 6, 14, 9, 11, 10)
    for spot_slot, cell_slot in zip(range(1, group), near_first):
        cell_copy(cell_slot).start()
        spot_copy(spot_slot).start()
    for slot in range(1, group):
        cell_copy(slot).wait()
        spot_copy(slot).wait()

    def half(by_row, by_lane, finish):
        highest[...] = jnp.full(highest.shape, lowest, jnp.float32)
        total[...] = jnp.zeros(total.shape, jnp.float32)

        def fill(step, tile):
            chunk, part = chunks - 1 - step // tiles, step % tiles
            left = by_row[pl.ds(pl.multiple_of(part * rows, rows), rows), :]
            right = by_lane[pl.ds(pl.multiple_of(chunk * lanes, lanes), lanes), :]
            scores = dot_last(left, right)
            tile[...] = scores
            return jnp.max(scores.reshape(rows // 8, 8, lanes), axis=0)

        def absorb(step, tile, newest):
            chunk = chunks - 1 - step // tiles
            before = highest[chunk]
            after = jnp.maximum(before, newest)
            highest[chunk] = after
            scores = tile[...].reshape(rows // 8, 8, lanes)
            total[chunk] = total[chunk] * jnp.exp(before - after) + jnp.sum(
                jnp.exp(scores - after[None]), axis=0
            )

        def close(chunk):
            top = jnp.max(highest[chunk], axis=0, keepdims=True)
            sums = jnp.sum(total[chunk] * jnp.exp(highest[chunk] - top), axis=0, keepdims=True)
            finish(chunk, top, sums)

        def body(pair, newest):
            step = 2 * pair
            second = fill(step + 1, tile_b)
            absorb(step, tile_a, newest)
            third = fill(step + 2, tile_a)
            absorb(step + 1, tile_b, second)

            @pl.when(pair % (tiles // 2) == tiles // 2 - 1)
            def _():
                close(chunks - 1 - (step + 1) // tiles)

            return third

        count = chunks * tiles
        newest = lax.fori_loop(0, count // 2 - 1, body, fill(0, tile_a))
        second = fill(count - 1, tile_b)
        absorb(count - 2, tile_a, newest)
        absorb(count - 1, tile_b, second)
        close(0)

    def store_pair(out, slot, top, sums, first):
        out[slot, 0:1, 0:width] = top[:, first:first + width]
        out[slot, 1:2, 0:width] = sums[:, first:first + width]

    def combine(part):
        top = part[0, 0:1, 0:width]
        for slot in range(1, group):
            top = jnp.maximum(top, part[slot, 0:1, 0:width])
        sums = jnp.zeros_like(top)
        for slot in range(group):
            sums += part[slot, 1:2, 0:width] * jnp.exp(part[slot, 0:1, 0:width] - top)
        return top + jnp.log(sums)

    def part_1_copy(slot, target):
        return pltpu.make_async_remote_copy(
            src_ref=out_1.at[slot],
            dst_ref=part_1.at[slot],
            send_sem=part_1_send.at[slot],
            recv_sem=part_1_recv.at[slot],
            device_id=target,
            device_id_type=MESH,
        )

    def finish_1(chunk, top, sums):
        store_pair(out_1, 2 * chunk + 1, top, sums, width)
        if isinstance(chunk, int):
            store_pair(part_1, 0, top, sums, 0)
            part_1_copy(1, along_q(0, 1)).start()
        else:
            store_pair(out_1, 2 * chunk, top, sums, 0)
            back = (8 - z_shift(chunk)) % 8
            part_1_copy(2 * chunk, along_q(back, 0)).start()
            part_1_copy(2 * chunk + 1, along_q(back, 1)).start()

    half(cells, spots, finish_1)
    for slot in range(1, group):
        part_1_copy(slot, along_q((8 - z_shift_of(slot // 2)) % 8, slot % 2)).wait()
    log_sum = combine(part_1)
    mass = spot_mass[...].reshape(1, width)
    log_count = math.log(256 * width)
    term = mass - log_sum + log_count
    spot_out[...] = (epsilon * (term + norms(spot_feat[...]))).reshape(width)
    dual[0] = term

    def dual_copy(slot):
        return pltpu.make_async_remote_copy(
            src_ref=dual.at[0],
            dst_ref=dual.at[slot],
            send_sem=dual_send.at[slot],
            recv_sem=dual_recv.at[slot],
            device_id=along_q(z_shift_of(slot // 2), slot % 2),
            device_id_type=MESH,
        )

    for slot in range(1, group):
        dual_copy(slot).start()
    keep = jnp.logical_not(lane_between(offset_lane, offset_lane + 6))
    for slot in range(group):
        if slot:
            dual_copy(slot).wait()
        at = slice(slot * width, (slot + 1) * width)
        moved = dot_first(pieces(dual[slot]), placing(16, dual_lane, 1.0))
        spots[at, :] = jnp.where(keep, spots[at, :].astype(jnp.float32), moved).astype(jnp.bfloat16)

    def part_2_copy(slot, target):
        return pltpu.make_async_remote_copy(
            src_ref=out_2.at[slot],
            dst_ref=part_2.at[slot],
            send_sem=part_2_send.at[slot],
            recv_sem=part_2_recv.at[slot],
            device_id=target,
            device_id_type=MESH,
        )

    def finish_2(chunk, top, sums):
        store_pair(out_2, 2 * chunk + 1, top, sums, width)
        if isinstance(chunk, int):
            store_pair(part_2, 0, top, sums, 0)
            part_2_copy(1, along_p(0, 3)).start()
        else:
            store_pair(out_2, 2 * chunk, top, sums, 0)
            back_x, near_y = (4 - chunk // 2) % 4, 2 * (chunk % 2)
            part_2_copy(2 * chunk, along_p(back_x, (4 - near_y) % 4)).start()
            part_2_copy(2 * chunk + 1, along_p(back_x, 3 - near_y)).start()

    half(spots, cells, finish_2)
    for slot in range(1, group):
        part_2_copy(slot, along_p((4 - slot // 4) % 4, (4 - slot % 4) % 4)).wait()
    log_sum = combine(part_2)
    mass = cell_mass[...].reshape(1, width)
    cell_out[...] = (epsilon * (mass - log_sum + norms(cell_feat[...]) + log_count)).reshape(width)


def local(*arguments):
    vmem = pl.BlockSpec(memory_space=pltpu.VMEM)
    points = group * width
    return pl.pallas_call(
        kernel,
        out_shape=[jax.ShapeDtypeStruct((width,), jnp.float32)] * 2,
        in_specs=[vmem] * 7,
        out_specs=[vmem] * 2,
        scratch_shapes=[
            pltpu.VMEM((points, depth), jnp.bfloat16),
            pltpu.VMEM((points, depth), jnp.bfloat16),
            pltpu.VMEM((rows, lanes), jnp.float32),
            pltpu.VMEM((rows, lanes), jnp.float32),
            pltpu.VMEM((chunks, 8, lanes), jnp.float32),
            pltpu.VMEM((chunks, 8, lanes), jnp.float32),
            pltpu.VMEM((group, 2, width), jnp.float32),
            pltpu.VMEM((group, 2, width), jnp.float32),
            pltpu.VMEM((group, 1, width), jnp.float32),
            pltpu.VMEM((group, 2, width), jnp.float32),
            pltpu.VMEM((group, 2, width), jnp.float32),
        ]
        + [pltpu.SemaphoreType.DMA((group,))] * 10,
        compiler_params=pltpu.CompilerParams(
            collective_id=0, has_side_effects=True, vmem_limit_bytes=32 * 1024 * 1024
        ),
        name="sweep",
    )(*arguments)


def solution(mesh):
    column = P(None, ("blk", "grp"))
    flat = P(("blk", "grp"))
    return jax.shard_map(
        local,
        mesh=mesh,
        in_specs=(column, column, flat, column, column, flat, flat),
        out_specs=(flat, flat),
        check_vma=False,
    )
```

time: 868 us -> 71.6 us (0.08)
  blocking collectives: 412 us -> 0 us
  waiting for transfers between devices: 212 us -> 0 us
  matrix products: 83.4 us -> 0 us
  local copies, waits for them, and re-layouts: 85.6 us -> 6.12 us
  Pallas kernels: 0 us -> 64.3 us
  other arithmetic: 54.5 us -> 0 us
  between operations: 14.3 us -> 0.66 us
    all_gather x12 -> x0, blocking collectives: 412 us -> none  [the longest x4 138 us: joined(): pieces = jax.tree.map(lambda part: lax.all_gather(part, axis), value)]
    unnamed x4 -> x0, waiting for transfers between devices: 212 us -> none
    dot_general x32 -> x0, matrix products: 83.4 us -> none  [contract(): lax.dot_general(left_side, right_side, (((0,), (0,)), ((), ())), preferre...]
    dynamic_slice x80 -> x0, local copies, waits for them, and re-layouts: 66 us -> none  [the longest x62 62.9 us: joined(): lax.scan(lambda so_far, section: (join(so_far, section), None), head, tail)]
    pallas_call x0 -> x1, Pallas kernels: none -> 64.3 us  [local(): pl.pallas_call(kernel, out_shape=[jax.ShapeDtypeStruct((width,), jnp.floa...]
    reduce_sum x20 -> x0, other arithmetic: 50.2 us -> none  [the longest x16 48.2 us: absorb(): jnp.sum(jnp.exp(scores - newest[:, None]), axis=1)]
  transfers between devices with their start and end apart: 2 -> 0, of which waited for: 2 -> 0; matrix products, arithmetic and copies ran while one was open for 2% -> 0% of each run, Pallas kernels for 0% -> 0%
where the time goes in v1:
time: 71.6 us; the launch traced here: 71.1 us
  Pallas kernels  64.3 us (90%)
  local copies, waits for them, and re-layouts  6.12 us (9%)
    pallas_call x1, Pallas kernels, local(): pl.pallas_call(kernel, out_shape=[jax.ShapeDtypeStruct((width,), jnp.floa...  64.3 us
    unnamed x16, local copies, waits for them, and re-layouts  6.12 us

profile of v1, /device:TPU:1, one launch (start us, length us, event | category | flops | bytes accessed | tf_op | source)
XLA Modules:
  0.0 71.1 jit_solution(17176274720858298709)
XLA Ops:
  0.6 0.0 copy-start
  0.6 0.7 %copy-done = bf16[64,192]{1,0:T(8,128)(2,1)S(1)} copy-done((bf16[64,192]{1,0:T(8,128)(2,1)S(1)}, bf16[64,192]{1,0:T(8,128)(2,1)}, u32[]{:S(2)}) %copy-start) | copy-done | bytes 24600
  1.4 0.0 copy-start.1
  1.4 0.8 %copy-done.1 = bf16[64,192]{1,0:T(8,128)(2,1)S(1)} copy-done((bf16[64,192]{1,0:T(8,128)(2,1)S(1)}, bf16[64,192]{1,0:T(8,128)(2,1)}, u32[]{:S(2)}) %copy-start.1) | copy-done | bytes 24600
  2.1 0.0 copy-start.2
  2.2 0.7 %copy-done.2 = bf16[34,192]{1,0:T(8,128)(2,1)S(1)} copy-done((bf16[34,192]{1,0:T(8,128)(2,1)S(1)}, bf16[34,192]{1,0:T(8,128)(2,1)}, u32[]{:S(2)}) %copy-start.2) | copy-done | bytes 13080
  2.9 0.0 copy-start.3
  2.9 0.7 %copy-done.3 = bf16[34,192]{1,0:T(8,128)(2,1)S(1)} copy-done((bf16[34,192]{1,0:T(8,128)(2,1)S(1)}, bf16[34,192]{1,0:T(8,128)(2,1)}, u32[]{:S(2)}) %copy-start.3) | copy-done | bytes 13080
  3.6 0.0 copy-start.4
  3.6 0.7 copy-done.4
  4.3 0.0 copy-start.5
  4.3 0.7 copy-done.5
  5.0 0.0 copy-start.6
  5.0 0.7 copy-done.6
  5.6 64.3 %sweep.1 = (f32[192]{0:T(256)S(1)}, f32[192]{0:T(256)S(1)}) custom-call(bf16[64,192]{1,0:T(8,128)(2,1)S(1)} %copy-done, bf16[34,192]{1,0:T(8,128)(2,1)S(1)} %copy-done.2, f32[192]{0:T(256)S(1)} %copy-done.4, bf16[64,192]{1,0:T(8,128)(2,1)S(1)} %copy-done.1, bf16[34,192]{1,0:T(8,128)(2,1)S(1)} %copy-done.3, f32[192]{0:T(256)S(1)} %copy-done.5, f32[192]{0:T(256)S(1)} %copy-done.6), custom_call_target="tpu_custom_call" | custom-call | tf_op jit(solution)/shard_map/sweep/pallas_call | solution.py:290
  69.9 0.6 copy.11
  70.5 0.6 copy.12
Async XLA Ops:
  0.6 0.8 %copy-start = (bf16[64,192]{1,0:T(8,128)(2,1)S(1)}, bf16[64,192]{1,0:T(8,128)(2,1)}, u32[]{:S(2)}) copy-start(bf16[64,192]{1,0:T(8,128)(2,1)} %spot_feat.1) | copy-start | bytes 73732
  1.4 0.8 %copy-start.1 = (bf16[64,192]{1,0:T(8,128)(2,1)S(1)}, bf16[64,192]{1,0:T(8,128)(2,1)}, u32[]{:S(2)}) copy-start(bf16[64,192]{1,0:T(8,128)(2,1)} %cell_feat.1) | copy-start | bytes 73732
  2.1 0.7 %copy-start.2 = (bf16[34,192]{1,0:T(8,128)(2,1)S(1)}, bf16[34,192]{1,0:T(8,128)(2,1)}, u32[]{:S(2)}) copy-start(bf16[34,192]{1,0:T(8,128)(2,1)} %spot_fac.1) | copy-start | bytes 39172
  2.9 0.7 %copy-start.3 = (bf16[34,192]{1,0:T(8,128)(2,1)S(1)}, bf16[34,192]{1,0:T(8,128)(2,1)}, u32[]{:S(2)}) copy-start(bf16[34,192]{1,0:T(8,128)(2,1)} %cell_fac.1) | copy-start | bytes 39172
  3.6 0.7 copy-start.4
  4.3 0.7 copy-start.5
  5.0 0.7 copy-start.6

commit v2 on v1

--- a/solution.py
+++ b/solution.py
@@ -68,10 +68,15 @@
     return (pair + 1) // 2 if pair % 2 else (8 - pair // 2) % 8
 
 
+def near(place):
+    return place + (place // 2) * (5 - 2 * place)
+
+
 def kernel(
-    spot_feat, spot_fac, spot_mass, cell_feat, cell_fac, cell_mass, cell_pot,
+    spot_feat_in, spot_fac_in, spot_mass_in, cell_feat_in, cell_fac_in, cell_mass_in, cell_pot_in,
     spot_out, cell_out,
-    spots, cells, tile_a, tile_b, highest, total,
+    spot_feat, spot_fac, spot_mass, cell_feat, cell_fac, cell_mass, cell_pot, input_sem,
+    spots, cells, spread, tile_a, tile_b, highest, total,
     part_1, out_1, dual, part_2, out_2,
     spot_send, spot_recv, cell_send, cell_recv,
     part_1_send, part_1_recv, dual_send, dual_recv, part_2_send, part_2_recv,
@@ -89,14 +94,27 @@
     def along_p(dx, dy):
         return place((my_x + dx) % 4, (my_y + dy) % 4, my_z, my_core)
 
+    loads = [
+        pltpu.make_async_copy(source, target, input_sem.at[at])
+        for at, (source, target) in enumerate((
+            (cell_feat_in, cell_feat), (cell_fac_in, cell_fac), (cell_pot_in, cell_pot),
+            (spot_feat_in, spot_feat), (spot_fac_in, spot_fac),
+            (spot_mass_in, spot_mass), (cell_mass_in, cell_mass),
+        ))
+    ]
+    for load in loads:
+        load.start()
+
     barrier = pltpu.get_barrier_semaphore()
     for slot in range(1, group):
         pl.semaphore_signal(
             barrier, inc=1, device_id=along_q(z_shift_of(slot // 2), slot % 2), device_id_type=MESH
         )
         pl.semaphore_signal(
-            barrier, inc=1, device_id=along_p(slot // 4, slot % 4), device_id_type=MESH
-        )
+            barrier, inc=1, device_id=along_p(near(slot // 4), near(slot % 4)), device_id_type=MESH
+        )
+    for load in loads:
+        load.wait()
 
     own_spots = (
         dot_first(spot_feat[...], placing(features, 0, 0.125))
@@ -114,15 +132,35 @@
     own_cells = jnp.where(lane_between(dual_lane, dual_lane + 3), 1.0, own_cells)
     cells[0:width, :] = own_cells.astype(jnp.bfloat16)
 
+    source = lax.broadcasted_iota(jnp.int32, spread.shape, 0)
+    target = lax.broadcasted_iota(jnp.int32, spread.shape, 1)
+    lane, kind = target % depth, source // group
+    value = jnp.where(
+        lane == dual_lane + kind,
+        jnp.where(kind < 3, 1.0, 0.0),
+        jnp.where((kind == 3) & (lane >= offset_lane) & (lane < dual_lane), -1.0, 0.0),
+    )
+    spread[...] = jnp.where(target // depth == source % group, value, 0.0).astype(jnp.bfloat16)
+
     pl.semaphore_wait(barrier, 2 * (group - 1))
 
-    def spot_copy(slot):
+    def spot_copy(pair):
         return pltpu.make_async_remote_copy(
             src_ref=spots.at[pl.ds(0, width), :],
-            dst_ref=spots.at[pl.ds(slot * width, width), :],
-            send_sem=spot_send.at[slot],
-            recv_sem=spot_recv.at[slot],
-            device_id=along_q(z_shift_of(slot // 2), slot % 2),
+            dst_ref=spots.at[pl.ds(2 * pair * width, width), :],
+            send_sem=spot_send.at[2 * pair],
+            recv_sem=spot_recv.at[2 * pair],
+            device_id=along_q(z_shift_of(pair), 0),
+            device_id_type=MESH,
+        )
+
+    def spot_pass(pair):
+        return pltpu.make_async_remote_copy(
+            src_ref=spots.at[pl.ds(2 * pair * width, width), :],
+            dst_ref=spots.at[pl.ds((2 * pair + 1) * width, width), :],
+            send_sem=spot_send.at[2 * pair + 1],
+            recv_sem=spot_recv.at[2 * pair + 1],
+            device_id=along_q(0, 1),
             device_id_type=MESH,
         )
 
@@ -132,64 +170,88 @@
             dst_ref=cells.at[pl.ds(slot * width, width), :],
             send_sem=cell_send.at[slot],
             recv_sem=cell_recv.at[slot],
-            device_id=along_p(slot // 4, slot % 4),
-            device_id_type=MESH,
-        )
-
-    near_first = (1, 3, 4, 12, 5, 7, 13, 15, 2, 8, 6, 14, 9, 11, 10)
-    for spot_slot, cell_slot in zip(range(1, group), near_first):
-        cell_copy(cell_slot).start()
-        spot_copy(spot_slot).start()
-    for slot in range(1, group):
-        cell_copy(slot).wait()
-        spot_copy(slot).wait()
-
-    def half(by_row, by_lane, finish):
+            device_id=along_p(near(slot // 4), near(slot % 4)),
+            device_id_type=MESH,
+        )
+
+    def pass_on(*pairs):
+        for pair in pairs:
+            spot_copy(pair).wait_recv()
+            spot_pass(pair).start()
+
+    spot_pass(0).start()
+    spot_copy(1).start()
+    for slot in range(1, 4):
+        cell_copy(slot).start()
+    for part in range(1, 4):
+        spot_copy(2 * part).start()
+        for slot in range(4 * part, 4 * part + 4):
+            cell_copy(slot).start()
+        spot_copy(2 * part + 1).start()
+
+    def arrive(part):
+        for slot in range(max(4 * part, 1), 4 * part + 4):
+            cell_copy(slot).wait_recv()
+        spot_pass(2 * part).wait_recv()
+        spot_pass(2 * part + 1).wait_recv()
+
+    def clear():
         highest[...] = jnp.full(highest.shape, lowest, jnp.float32)
         total[...] = jnp.zeros(total.shape, jnp.float32)
 
-        def fill(step, tile):
-            chunk, part = chunks - 1 - step // tiles, step % tiles
-            left = by_row[pl.ds(pl.multiple_of(part * rows, rows), rows), :]
-            right = by_lane[pl.ds(pl.multiple_of(chunk * lanes, lanes), lanes), :]
-            scores = dot_last(left, right)
-            tile[...] = scores
-            return jnp.max(scores.reshape(rows // 8, 8, lanes), axis=0)
-
-        def absorb(step, tile, newest):
-            chunk = chunks - 1 - step // tiles
-            before = highest[chunk]
-            after = jnp.maximum(before, newest)
-            highest[chunk] = after
-            scores = tile[...].reshape(rows // 8, 8, lanes)
-            total[chunk] = total[chunk] * jnp.exp(before - after) + jnp.sum(
-                jnp.exp(scores - after[None]), axis=0
-            )
-
-        def close(chunk):
-            top = jnp.max(highest[chunk], axis=0, keepdims=True)
-            sums = jnp.sum(total[chunk] * jnp.exp(highest[chunk] - top), axis=0, keepdims=True)
-            finish(chunk, top, sums)
+    def fill(by_row, by_lane, part, chunk, tile):
+        left = by_row[pl.ds(pl.multiple_of(part * rows, rows), rows), :]
+        right = by_lane[pl.ds(pl.multiple_of(chunk * lanes, lanes), lanes), :]
+        scores = dot_last(left, right)
+        tile[...] = scores
+        return jnp.max(scores.reshape(rows // 8, 8, lanes), axis=0)
+
+    def absorb(chunk, tile, newest):
+        before = highest[chunk]
+        after = jnp.maximum(before, newest)
+        highest[chunk] = after
+        scores = tile[...].reshape(rows // 8, 8, lanes)
+        total[chunk] = total[chunk] * jnp.exp(before - after) + jnp.sum(
+            jnp.exp(scores - after[None]), axis=0
+        )
+
+    def close(chunk, finish):
+        top = jnp.max(highest[chunk], axis=0, keepdims=True)
+        sums = jnp.sum(total[chunk] * jnp.exp(highest[chunk] - top), axis=0, keepdims=True)
+        finish(chunk, top, sums)
+
+    count = chunks * tiles
+
+    def half(by_row, by_lane, plan, closes, events, finish):
+        clear()
 
         def body(pair, newest):
             step = 2 * pair
-            second = fill(step + 1, tile_b)
-            absorb(step, tile_a, newest)
-            third = fill(step + 2, tile_a)
-            absorb(step + 1, tile_b, second)
-
-            @pl.when(pair % (tiles // 2) == tiles // 2 - 1)
+            second = fill(by_row, by_lane, *plan(step + 1), tile_b)
+            absorb(plan(step)[1], tile_a, newest)
+            for at, event in events:
+                pl.when(pair == at)(event)
+            third = fill(by_row, by_lane, *plan(step + 2), tile_a)
+            absorb(plan(step + 1)[1], tile_b, second)
+
+            @pl.when(closes(step))
             def _():
-                close(chunks - 1 - (step + 1) // tiles)
+                close(plan(step)[1], finish)
+
+            @pl.when(closes(step + 1))
+            def _():
+                close(plan(step + 1)[1], finish)
 
             return third
 
-        count = chunks * tiles
-        newest = lax.fori_loop(0, count // 2 - 1, body, fill(0, tile_a))
-        second = fill(count - 1, tile_b)
-        absorb(count - 2, tile_a, newest)
-        absorb(count - 1, tile_b, second)
-        close(0)
+        part, chunk = plan(0)
+        newest = lax.fori_loop(0, count // 2 - 1, body, fill(by_row, by_lane, part, chunk, tile_a))
+        second = fill(by_row, by_lane, *plan(count - 1), tile_b)
+        absorb(plan(count - 2)[1], tile_a, newest)
+        if closes(count - 2):
+            close(plan(count - 2)[1], finish)
+        absorb(0, tile_b, second)
+        close(0, finish)
 
     def store_pair(out, slot, top, sums, first):
         out[slot, 0:1, 0:width] = top[:, first:first + width]
@@ -225,20 +287,50 @@
             part_1_copy(2 * chunk, along_q(back, 0)).start()
             part_1_copy(2 * chunk + 1, along_q(back, 1)).start()
 
-    half(cells, spots, finish_1)
+    def plan_1(step):
+        turn = sum(jnp.where(step >= 2 * k * k, 1, 0) for k in range(1, tiles))
+        rest = step - 2 * turn * turn
+        old = rest < 2 * turn
+        part = jnp.where(old, jnp.where(rest < turn, rest, rest - turn), turn)
+        chunk = jnp.where(
+            old, 2 * turn + jnp.where(rest < turn, 0, 1), 4 * turn + 1 - rest
+        )
+        return part, chunk
+
+    pass_on(1)
+    arrive(0)
+    half(
+        cells,
+        spots,
+        plan_1,
+        lambda step: step >= count - chunks,
+        (
+            (0, lambda: (pass_on(2, 3), arrive(1), None)[-1]),
+            (1, lambda: pass_on(4, 5)),
+            (3, lambda: arrive(2)),
+            (5, lambda: pass_on(6, 7)),
+            (8, lambda: arrive(3)),
+        ),
+        finish_1,
+    )
+    for pair in range(8):
+        spot_pass(pair).wait_send()
+        if pair:
+            spot_copy(pair).wait_send()
     for slot in range(1, group):
+        cell_copy(slot).wait_send()
         part_1_copy(slot, along_q((8 - z_shift_of(slot // 2)) % 8, slot % 2)).wait()
     log_sum = combine(part_1)
     mass = spot_mass[...].reshape(1, width)
     log_count = math.log(256 * width)
     term = mass - log_sum + log_count
     spot_out[...] = (epsilon * (term + norms(spot_feat[...]))).reshape(width)
-    dual[0] = term
+    dual[0:1, :] = term
 
     def dual_copy(slot):
         return pltpu.make_async_remote_copy(
-            src_ref=dual.at[0],
-            dst_ref=dual.at[slot],
+            src_ref=dual.at[pl.ds(0, 1), :],
+            dst_ref=dual.at[pl.ds(slot, 1), :],
             send_sem=dual_send.at[slot],
             recv_sem=dual_recv.at[slot],
             device_id=along_q(z_shift_of(slot // 2), slot % 2),
@@ -247,13 +339,17 @@
 
     for slot in range(1, group):
         dual_copy(slot).start()
-    keep = jnp.logical_not(lane_between(offset_lane, offset_lane + 6))
+    for slot in range(1, group):
+        dual_copy(slot).wait()
+    values = dual[...]
+    high = values.astype(jnp.bfloat16).astype(jnp.float32)
+    middle = (values - high).astype(jnp.bfloat16).astype(jnp.float32)
+    low = values - high - middle
+    stacked = jnp.concatenate([high, middle, low, jnp.ones_like(low)], axis=0).astype(jnp.bfloat16)
+    moved = dot_first(stacked, spread[...]).astype(jnp.bfloat16)
     for slot in range(group):
-        if slot:
-            dual_copy(slot).wait()
         at = slice(slot * width, (slot + 1) * width)
-        moved = dot_first(pieces(dual[slot]), placing(16, dual_lane, 1.0))
-        spots[at, :] = jnp.where(keep, spots[at, :].astype(jnp.float32), moved).astype(jnp.bfloat16)
+        spots[at, :] = spots[at, :] + moved[:, slot * depth:(slot + 1) * depth]
 
     def part_2_copy(slot, target):
         return pltpu.make_async_remote_copy(
@@ -272,13 +368,16 @@
             part_2_copy(1, along_p(0, 3)).start()
         else:
             store_pair(out_2, 2 * chunk, top, sums, 0)
-            back_x, near_y = (4 - chunk // 2) % 4, 2 * (chunk % 2)
-            part_2_copy(2 * chunk, along_p(back_x, (4 - near_y) % 4)).start()
-            part_2_copy(2 * chunk + 1, along_p(back_x, 3 - near_y)).start()
-
-    half(spots, cells, finish_2)
+            back_x, first_y = (4 - near(chunk // 2)) % 4, 2 * (chunk % 2)
+            part_2_copy(2 * chunk, along_p(back_x, (4 - near(first_y)) % 4)).start()
+            part_2_copy(2 * chunk + 1, along_p(back_x, (4 - near(first_y + 1)) % 4)).start()
+
+    def plan_2(step):
+        return step % tiles, chunks - 1 - step // tiles
+
+    half(spots, cells, plan_2, lambda step: step % tiles == tiles - 1, (), finish_2)
     for slot in range(1, group):
-        part_2_copy(slot, along_p((4 - slot // 4) % 4, (4 - slot % 4) % 4)).wait()
+        part_2_copy(slot, along_p((4 - near(slot // 4)) % 4, (4 - near(slot % 4)) % 4)).wait()
     log_sum = combine(part_2)
     mass = cell_mass[...].reshape(1, width)
     cell_out[...] = (epsilon * (mass - log_sum + norms(cell_feat[...]) + log_count)).reshape(width)
@@ -290,24 +389,27 @@
     return pl.pallas_call(
         kernel,
         out_shape=[jax.ShapeDtypeStruct((width,), jnp.float32)] * 2,
-        in_specs=[vmem] * 7,
+        in_specs=[pl.BlockSpec(memory_space=pl.ANY)] * 7,
         out_specs=[vmem] * 2,
-        scratch_shapes=[
+        scratch_shapes=[pltpu.VMEM(value.shape, value.dtype) for value in arguments]
+        + [
+            pltpu.SemaphoreType.DMA((7,)),
             pltpu.VMEM((points, depth), jnp.bfloat16),
             pltpu.VMEM((points, depth), jnp.bfloat16),
+            pltpu.VMEM((4 * group, group * depth), jnp.bfloat16),
             pltpu.VMEM((rows, lanes), jnp.float32),
             pltpu.VMEM((rows, lanes), jnp.float32),
             pltpu.VMEM((chunks, 8, lanes), jnp.float32),
             pltpu.VMEM((chunks, 8, lanes), jnp.float32),
             pltpu.VMEM((group, 2, width), jnp.float32),
             pltpu.VMEM((group, 2, width), jnp.float32),
-            pltpu.VMEM((group, 1, width), jnp.float32),
+            pltpu.VMEM((group, width), jnp.float32),
             pltpu.VMEM((group, 2, width), jnp.float32),
             pltpu.VMEM((group, 2, width), jnp.float32),
         ]
         + [pltpu.SemaphoreType.DMA((group,))] * 10,
         compiler_params=pltpu.CompilerParams(
-            collective_id=0, has_side_effects=True, vmem_limit_bytes=32 * 1024 * 1024
+            collective_id=0, has_side_effects=True, vmem_limit_bytes=56 * 1024 * 1024
         ),
         name="sweep",
     )(*arguments)

time: 71.6 us -> 61.6 us (0.86)
  Pallas kernels: 64.3 us -> 58.5 us
  local copies, waits for them, and re-layouts: 6.12 us -> 1.86 us
    pallas_call x1, Pallas kernels: 64.3 us -> 58.5 us  [local(): pl.pallas_call(kernel, out_shape=[jax.ShapeDtypeStruct((width,), jnp.floa...]
    unnamed x16 -> x6, local copies, waits for them, and re-layouts: 6.12 us -> 1.86 us
where the time goes in v2:
time: 61.6 us; the launch traced here: 61 us
  Pallas kernels  58.5 us (95%)
  local copies, waits for them, and re-layouts  1.86 us (3%)
  between operations  0.65 us (1%)
    pallas_call x1, Pallas kernels, local(): pl.pallas_call(kernel, out_shape=[jax.ShapeDtypeStruct((width,), jnp.floa...  58.5 us
    unnamed x6, local copies, waits for them, and re-layouts  1.86 us

profile of v2, /device:TPU:1, one launch (start us, length us, event | category | flops | bytes accessed | tf_op | source)
XLA Modules:
  0.0 61.0 jit_solution(15161533216903489592)
XLA Ops:
  0.6 58.5 %sweep.1 = (f32[192]{0:T(256)}, f32[192]{0:T(256)}) custom-call(bf16[64,192]{1,0:T(8,128)(2,1)} %spot_feat_in.1, bf16[34,192]{1,0:T(8,128)(2,1)} %spot_fac_in.1, f32[192]{0:T(256)} %spot_mass_in.1, bf16[64,192]{1,0:T(8,128)(2,1)} %cell_feat_in.1, bf16[34,192]{1,0:T(8,128)(2,1)} %cell_fac_in.1, f32[192]{0:T(256)} %cell_mass_in.1, f32[192]{0:T(256)} %cell_pot_in.1), custom_call_target="tpu_custom_call" | custom-call | tf_op jit(solution)/shard_map/sweep/pallas_call | solution.py:389
  59.1 0.0 copy-start.1
  59.2 0.7 %copy-done.1 = f32[192]{0:T(256)S(1)} copy-done((f32[192]{0:T(256)S(1)}, f32[192]{0:T(256)}, u32[]{:S(2)}) %copy-start.1) | copy-done | bytes 792
  59.8 0.0 copy-start
  59.8 0.6 copy.11
  60.4 0.1 copy-done
  60.5 0.6 copy.12
Async XLA Ops:
  59.1 0.7 %copy-start.1 = (f32[192]{0:T(256)S(1)}, f32[192]{0:T(256)}, u32[]{:S(2)}) copy-start(f32[192]{0:T(256)} %get-tuple-element.4) | copy-start | bytes 2308
  59.8 0.6 %copy-start = (f32[192]{0:T(256)S(1)}, f32[192]{0:T(256)}, u32[]{:S(2)}) copy-start(f32[192]{0:T(256)} %get-tuple-element.5) | copy-start | bytes 2308

commit v3 on v2

--- a/solution.py
+++ b/solution.py
@@ -14,10 +14,12 @@
 offset_lane = features + factors
 dual_lane = offset_lane + 3
 group = 16
-rows = 768
 lanes = 384
 chunks = group * width // lanes
-tiles = group * width // rows
+near_rows = 7 * width
+far_rows = 9 * width
+half_rows = group * width // 2
+part_rows = width // 2
 lowest = -1e30
 MESH = pl.DeviceIdType.MESH
 
@@ -68,8 +70,20 @@
     return (pair + 1) // 2 if pair % 2 else (8 - pair // 2) % 8
 
 
-def near(place):
+def shift(place):
     return place + (place // 2) * (5 - 2 * place)
+
+
+def slot_of(i, j):
+    if j == 0:
+        return i
+    return 3 + j if i == 0 else 7 + 3 * (j - 1) + i - 1
+
+
+def lines_of(slot):
+    i = jnp.where(slot < 4, slot, jnp.where(slot < 7, 0, 1 + (slot + 2) % 3))
+    j = jnp.where(slot < 4, 0, jnp.where(slot < 7, slot - 3, 1 + (slot - 7) // 3))
+    return i, j
 
 
 def kernel(
@@ -111,7 +125,7 @@
             barrier, inc=1, device_id=along_q(z_shift_of(slot // 2), slot % 2), device_id_type=MESH
         )
         pl.semaphore_signal(
-            barrier, inc=1, device_id=along_p(near(slot // 4), near(slot % 4)), device_id_type=MESH
+            barrier, inc=1, device_id=along_p(shift(slot // 4), shift(slot % 4)), device_id_type=MESH
         )
     for load in loads:
         load.wait()
@@ -144,13 +158,15 @@
 
     pl.semaphore_wait(barrier, 2 * (group - 1))
 
-    def spot_copy(pair):
-        return pltpu.make_async_remote_copy(
-            src_ref=spots.at[pl.ds(0, width), :],
-            dst_ref=spots.at[pl.ds(2 * pair * width, width), :],
-            send_sem=spot_send.at[2 * pair],
-            recv_sem=spot_recv.at[2 * pair],
-            device_id=along_q(z_shift_of(pair), 0),
+    def spot_copy(pair, source=0, first=0, count=width, flight=None):
+        target = z_shift_of(pair) - z_shift_of(source)
+        at = 2 * pair if flight is None else flight
+        return pltpu.make_async_remote_copy(
+            src_ref=spots.at[pl.ds(2 * source * width + first, count), :],
+            dst_ref=spots.at[pl.ds(2 * pair * width + first, count), :],
+            send_sem=spot_send.at[at],
+            recv_sem=spot_recv.at[at],
+            device_id=along_q((target + 8) % 8, 0),
             device_id_type=MESH,
         )
 
@@ -164,53 +180,92 @@
             device_id_type=MESH,
         )
 
-    def cell_copy(slot):
+    def cell_copy(i, j):
+        slot = slot_of(i, j)
         return pltpu.make_async_remote_copy(
             src_ref=cells.at[pl.ds(0, width), :],
             dst_ref=cells.at[pl.ds(slot * width, width), :],
             send_sem=cell_send.at[slot],
             recv_sem=cell_recv.at[slot],
-            device_id=along_p(near(slot // 4), near(slot % 4)),
-            device_id_type=MESH,
-        )
-
-    def pass_on(*pairs):
-        for pair in pairs:
-            spot_copy(pair).wait_recv()
-            spot_pass(pair).start()
-
-    spot_pass(0).start()
-    spot_copy(1).start()
-    for slot in range(1, 4):
-        cell_copy(slot).start()
-    for part in range(1, 4):
-        spot_copy(2 * part).start()
-        for slot in range(4 * part, 4 * part + 4):
-            cell_copy(slot).start()
-        spot_copy(2 * part + 1).start()
-
-    def arrive(part):
-        for slot in range(max(4 * part, 1), 4 * part + 4):
-            cell_copy(slot).wait_recv()
-        spot_pass(2 * part).wait_recv()
-        spot_pass(2 * part + 1).wait_recv()
+            device_id=along_p(shift(i), shift(j)),
+            device_id_type=MESH,
+        )
+
+    def cell_turn(i, j, along_y):
+        source, first = (slot_of(i, 0), 0) if along_y else (slot_of(0, j), part_rows)
+        at = slot_of(i, j) + (0 if along_y else 9)
+        return pltpu.make_async_remote_copy(
+            src_ref=cells.at[pl.ds(source * width + first, part_rows), :],
+            dst_ref=cells.at[pl.ds(slot_of(i, j) * width + first, part_rows), :],
+            send_sem=cell_send.at[at],
+            recv_sem=cell_recv.at[at],
+            device_id=along_p(0, shift(j)) if along_y else along_p(shift(i), 0),
+            device_id_type=MESH,
+        )
+
+    line = (1, 2, 3)
+    spot_direct = [spot_copy(pair) for pair in (3, 4, 1, 2)]
+    spot_further = [
+        spot_copy(5, 3),
+        spot_copy(6, 4),
+        spot_copy(7, 3, 0, part_rows),
+        spot_copy(7, 4, part_rows, part_rows, 16),
+    ]
+    cell_direct = [cell_copy(0, j) for j in line] + [cell_copy(i, 0) for i in line]
+    cell_turns = [
+        cell_turn(i, j, along_y) for i in line for j in line for along_y in (True, False)
+    ]
+    passes = [spot_pass(pair) for pair in range(8)]
+    passes[0].start()
+    for spot_step, cell_step in zip(spot_direct, ((0, 3), (1, 4), (2,), (5,))):
+        spot_step.start()
+        for at in cell_step:
+            cell_direct[at].start()
+    for i in line:
+        cell_copy(i, 0).wait_recv()
+        for j in line:
+            cell_turn(i, j, True).start()
+        cell_copy(0, i).wait_recv()
+        for j in line:
+            cell_turn(j, i, False).start()
+    for pair in (3, 4):
+        spot_copy(pair).wait_recv()
+    for step in spot_further:
+        step.start()
+    for pair in (1, 2):
+        spot_copy(pair).wait_recv()
+    for pair in range(1, 5):
+        passes[pair].start()
+    for pair in range(5):
+        passes[pair].wait_recv()
+
+    def further():
+        for step in spot_further:
+            step.wait_recv()
+        for pair in (5, 6, 7):
+            passes[pair].start()
+        for step in cell_turns:
+            step.wait_recv()
+
+    def sent():
+        for step in spot_direct + spot_further + cell_direct + cell_turns + passes:
+            step.wait_send()
 
     def clear():
         highest[...] = jnp.full(highest.shape, lowest, jnp.float32)
         total[...] = jnp.zeros(total.shape, jnp.float32)
 
-    def fill(by_row, by_lane, part, chunk, tile):
-        left = by_row[pl.ds(pl.multiple_of(part * rows, rows), rows), :]
+    def fill(by_row, first, count, by_lane, chunk, tile):
         right = by_lane[pl.ds(pl.multiple_of(chunk * lanes, lanes), lanes), :]
-        scores = dot_last(left, right)
-        tile[...] = scores
-        return jnp.max(scores.reshape(rows // 8, 8, lanes), axis=0)
-
-    def absorb(chunk, tile, newest):
+        scores = dot_last(by_row[pl.ds(first, count), :], right)
+        tile[0:count, :] = scores
+        return jnp.max(scores.reshape(count // 8, 8, lanes), axis=0)
+
+    def absorb(chunk, count, tile, newest):
         before = highest[chunk]
         after = jnp.maximum(before, newest)
         highest[chunk] = after
-        scores = tile[...].reshape(rows // 8, 8, lanes)
+        scores = tile[0:count, :].reshape(count // 8, 8, lanes)
         total[chunk] = total[chunk] * jnp.exp(before - after) + jnp.sum(
             jnp.exp(scores - after[None]), axis=0
         )
@@ -219,39 +274,6 @@
         top = jnp.max(highest[chunk], axis=0, keepdims=True)
         sums = jnp.sum(total[chunk] * jnp.exp(highest[chunk] - top), axis=0, keepdims=True)
         finish(chunk, top, sums)
-
-    count = chunks * tiles
-
-    def half(by_row, by_lane, plan, closes, events, finish):
-        clear()
-
-        def body(pair, newest):
-            step = 2 * pair
-            second = fill(by_row, by_lane, *plan(step + 1), tile_b)
-            absorb(plan(step)[1], tile_a, newest)
-            for at, event in events:
-                pl.when(pair == at)(event)
-            third = fill(by_row, by_lane, *plan(step + 2), tile_a)
-            absorb(plan(step + 1)[1], tile_b, second)
-
-            @pl.when(closes(step))
-            def _():
-                close(plan(step)[1], finish)
-
-            @pl.when(closes(step + 1))
-            def _():
-                close(plan(step + 1)[1], finish)
-
-            return third
-
-        part, chunk = plan(0)
-        newest = lax.fori_loop(0, count // 2 - 1, body, fill(by_row, by_lane, part, chunk, tile_a))
-        second = fill(by_row, by_lane, *plan(count - 1), tile_b)
-        absorb(plan(count - 2)[1], tile_a, newest)
-        if closes(count - 2):
-            close(plan(count - 2)[1], finish)
-        absorb(0, tile_b, second)
-        close(0, finish)
 
     def store_pair(out, slot, top, sums, first):
         out[slot, 0:1, 0:width] = top[:, first:first + width]
@@ -278,7 +300,7 @@
 
     def finish_1(chunk, top, sums):
         store_pair(out_1, 2 * chunk + 1, top, sums, width)
-        if isinstance(chunk, int):
+        if isinstance(chunk, int) and chunk == 0:
             store_pair(part_1, 0, top, sums, 0)
             part_1_copy(1, along_q(0, 1)).start()
         else:
@@ -287,38 +309,57 @@
             part_1_copy(2 * chunk, along_q(back, 0)).start()
             part_1_copy(2 * chunk + 1, along_q(back, 1)).start()
 
-    def plan_1(step):
-        turn = sum(jnp.where(step >= 2 * k * k, 1, 0) for k in range(1, tiles))
-        rest = step - 2 * turn * turn
-        old = rest < 2 * turn
-        part = jnp.where(old, jnp.where(rest < turn, rest, rest - turn), turn)
-        chunk = jnp.where(
-            old, 2 * turn + jnp.where(rest < turn, 0, 1), 4 * turn + 1 - rest
-        )
-        return part, chunk
-
-    pass_on(1)
-    arrive(0)
-    half(
-        cells,
-        spots,
-        plan_1,
-        lambda step: step >= count - chunks,
-        (
-            (0, lambda: (pass_on(2, 3), arrive(1), None)[-1]),
-            (1, lambda: pass_on(4, 5)),
-            (3, lambda: arrive(2)),
-            (5, lambda: pass_on(6, 7)),
-            (8, lambda: arrive(3)),
-        ),
-        finish_1,
-    )
-    for pair in range(8):
-        spot_pass(pair).wait_send()
-        if pair:
-            spot_copy(pair).wait_send()
+    def fill_near(chunk, tile):
+        return fill(cells, 0, near_rows, spots, chunk, tile)
+
+    def fill_far(chunk, tile):
+        return fill(cells, near_rows, far_rows, spots, chunk, tile)
+
+    def absorb_near(chunk, tile, newest):
+        absorb(chunk, near_rows, tile, newest)
+
+    def absorb_far(chunk, tile, newest):
+        absorb(chunk, far_rows, tile, newest)
+        close(chunk, finish_1)
+
+    clear()
+
+    def first_tiles(step, newest):
+        chunk = 2 * step
+        second = fill_near(chunk + 1, tile_b)
+        absorb_near(chunk, tile_a, newest)
+        third = fill_near(chunk + 2, tile_a)
+        absorb_near(chunk + 1, tile_b, second)
+        return third
+
+    newest = lax.fori_loop(0, 2, first_tiles, fill_near(0, tile_a))
+    further()
+    second = fill_far(4, tile_b)
+    absorb_near(4, tile_a, newest)
+    newest = fill_far(3, tile_a)
+    absorb_far(4, tile_b, second)
+    second = fill_far(2, tile_b)
+    absorb_far(3, tile_a, newest)
+    newest = fill_far(1, tile_a)
+    absorb_far(2, tile_b, second)
+    for pair in (5, 6, 7):
+        passes[pair].wait_recv()
+
+    def last_tiles(step, newest):
+        chunk = 5 + step
+        second = fill_near(chunk, tile_b)
+        absorb_far(jnp.where(step == 0, 1, chunk - 1), tile_a, newest)
+        third = fill_far(chunk, tile_a)
+        absorb_near(chunk, tile_b, second)
+        return third
+
+    newest = lax.fori_loop(0, 3, last_tiles, newest)
+    second = fill_far(0, tile_b)
+    absorb_far(7, tile_a, newest)
+    absorb_far(0, tile_b, second)
+
+    sent()
     for slot in range(1, group):
-        cell_copy(slot).wait_send()
         part_1_copy(slot, along_q((8 - z_shift_of(slot // 2)) % 8, slot % 2)).wait()
     log_sum = combine(part_1)
     mass = spot_mass[...].reshape(1, width)
@@ -361,23 +402,41 @@
             device_id_type=MESH,
         )
 
+    def owner(slot):
+        i, j = lines_of(slot)
+        return along_p((4 - shift(i)) % 4, (4 - shift(j)) % 4)
+
     def finish_2(chunk, top, sums):
         store_pair(out_2, 2 * chunk + 1, top, sums, width)
-        if isinstance(chunk, int):
+        if isinstance(chunk, int) and chunk == 0:
             store_pair(part_2, 0, top, sums, 0)
-            part_2_copy(1, along_p(0, 3)).start()
+            part_2_copy(1, owner(1)).start()
         else:
             store_pair(out_2, 2 * chunk, top, sums, 0)
-            back_x, first_y = (4 - near(chunk // 2)) % 4, 2 * (chunk % 2)
-            part_2_copy(2 * chunk, along_p(back_x, (4 - near(first_y)) % 4)).start()
-            part_2_copy(2 * chunk + 1, along_p(back_x, (4 - near(first_y + 1)) % 4)).start()
-
-    def plan_2(step):
-        return step % tiles, chunks - 1 - step // tiles
-
-    half(spots, cells, plan_2, lambda step: step % tiles == tiles - 1, (), finish_2)
+            part_2_copy(2 * chunk, owner(2 * chunk)).start()
+            part_2_copy(2 * chunk + 1, owner(2 * chunk + 1)).start()
+
+    clear()
+
+    def fill_2(part, chunk, tile):
+        return fill(spots, part * half_rows, half_rows, cells, chunk, tile)
+
+    def both(step, newest):
+        chunk = chunks - 1 - step
+        second = fill_2(1, chunk, tile_b)
+        absorb(chunk, half_rows, tile_a, newest)
+        third = fill_2(0, chunk - 1, tile_a)
+        absorb(chunk, half_rows, tile_b, second)
+        close(chunk, finish_2)
+        return third
+
+    newest = lax.fori_loop(0, chunks - 1, both, fill_2(0, chunks - 1, tile_a))
+    second = fill_2(1, 0, tile_b)
+    absorb(0, half_rows, tile_a, newest)
+    absorb(0, half_rows, tile_b, second)
+    close(0, finish_2)
     for slot in range(1, group):
-        part_2_copy(slot, along_p((4 - near(slot // 4)) % 4, (4 - near(slot % 4)) % 4)).wait()
+        part_2_copy(slot, owner(slot)).wait()
     log_sum = combine(part_2)
     mass = cell_mass[...].reshape(1, width)
     cell_out[...] = (epsilon * (mass - log_sum + norms(cell_feat[...]) + log_count)).reshape(width)
@@ -397,8 +456,8 @@
             pltpu.VMEM((points, depth), jnp.bfloat16),
             pltpu.VMEM((points, depth), jnp.bfloat16),
             pltpu.VMEM((4 * group, group * depth), jnp.bfloat16),
-            pltpu.VMEM((rows, lanes), jnp.float32),
-            pltpu.VMEM((rows, lanes), jnp.float32),
+            pltpu.VMEM((far_rows, lanes), jnp.float32),
+            pltpu.VMEM((far_rows, lanes), jnp.float32),
             pltpu.VMEM((chunks, 8, lanes), jnp.float32),
             pltpu.VMEM((chunks, 8, lanes), jnp.float32),
             pltpu.VMEM((group, 2, width), jnp.float32),
@@ -407,7 +466,8 @@
             pltpu.VMEM((group, 2, width), jnp.float32),
             pltpu.VMEM((group, 2, width), jnp.float32),
         ]
-        + [pltpu.SemaphoreType.DMA((group,))] * 10,
+        + [pltpu.SemaphoreType.DMA((count,)) for count in (17, 17, 25, 25)]
+        + [pltpu.SemaphoreType.DMA((group,))] * 6,
         compiler_params=pltpu.CompilerParams(
             collective_id=0, has_side_effects=True, vmem_limit_bytes=56 * 1024 * 1024
         ),

time: 61.6 us -> 57.7 us (0.937)
  Pallas kernels: 58.5 us -> 55 us
    pallas_call x1, Pallas kernels: 58.5 us -> 55 us  [local(): pl.pallas_call(kernel, out_shape=[jax.ShapeDtypeStruct((width,), jnp.floa...]
where the time goes in v3:
time: 57.7 us; the launch traced here: 57.5 us
  Pallas kernels  55 us (95%)
  local copies, waits for them, and re-layouts  1.86 us (3%)
  between operations  0.65 us (1%)
    pallas_call x1, Pallas kernels, local(): pl.pallas_call(kernel, out_shape=[jax.ShapeDtypeStruct((width,), jnp.floa...  55 us
    unnamed x6, local copies, waits for them, and re-layouts  1.86 us

profile of v3, /device:TPU:1, one launch (start us, length us, event | category | flops | bytes accessed | tf_op | source)
XLA Modules:
  0.0 57.5 jit_solution(8633416446084212773)
XLA Ops:
  0.6 55.0 %sweep.1 = (f32[192]{0:T(256)}, f32[192]{0:T(256)}) custom-call(bf16[64,192]{1,0:T(8,128)(2,1)} %spot_feat_in.1, bf16[34,192]{1,0:T(8,128)(2,1)} %spot_fac_in.1, f32[192]{0:T(256)} %spot_mass_in.1, bf16[64,192]{1,0:T(8,128)(2,1)} %cell_feat_in.1, bf16[34,192]{1,0:T(8,128)(2,1)} %cell_fac_in.1, f32[192]{0:T(256)} %cell_mass_in.1, f32[192]{0:T(256)} %cell_pot_in.1), custom_call_target="tpu_custom_call" | custom-call | tf_op jit(solution)/shard_map/sweep/pallas_call | solution.py:448
  55.6 0.0 copy-start.1
  55.6 0.7 %copy-done.1 = f32[192]{0:T(256)S(1)} copy-done((f32[192]{0:T(256)S(1)}, f32[192]{0:T(256)}, u32[]{:S(2)}) %copy-start.1) | copy-done | bytes 792
  56.3 0.0 copy-start
  56.3 0.6 copy.11
  56.9 0.1 copy-done
  56.9 0.6 copy.12
Async XLA Ops:
  55.6 0.7 %copy-start.1 = (f32[192]{0:T(256)S(1)}, f32[192]{0:T(256)}, u32[]{:S(2)}) copy-start(f32[192]{0:T(256)} %get-tuple-element.4) | copy-start | bytes 2308
  56.3 0.6 %copy-start = (f32[192]{0:T(256)S(1)}, f32[192]{0:T(256)}, u32[]{:S(2)}) copy-start(f32[192]{0:T(256)} %get-tuple-element.5) | copy-start | bytes 2308

commit v4 on v3

--- a/solution.py
+++ b/solution.py
@@ -120,13 +120,15 @@
         load.start()
 
     barrier = pltpu.get_barrier_semaphore()
-    for slot in range(1, group):
-        pl.semaphore_signal(
-            barrier, inc=1, device_id=along_q(z_shift_of(slot // 2), slot % 2), device_id_type=MESH
-        )
-        pl.semaphore_signal(
-            barrier, inc=1, device_id=along_p(shift(slot // 4), shift(slot % 4)), device_id_type=MESH
-        )
+    line = (1, 2, 3)
+    partners = (
+        [along_q(0, 1)]
+        + [along_q(z_shift_of(pair), 0) for pair in range(1, 5)]
+        + [along_p(shift(i), 0) for i in line]
+        + [along_p(0, shift(j)) for j in line]
+    )
+    for partner in partners:
+        pl.semaphore_signal(barrier, inc=1, device_id=partner, device_id_type=MESH)
     for load in loads:
         load.wait()
 
@@ -148,15 +150,15 @@
 
     source = lax.broadcasted_iota(jnp.int32, spread.shape, 0)
     target = lax.broadcasted_iota(jnp.int32, spread.shape, 1)
-    lane, kind = target % depth, source // group
+    lane, kind = target % depth, source // 8
     value = jnp.where(
         lane == dual_lane + kind,
         jnp.where(kind < 3, 1.0, 0.0),
         jnp.where((kind == 3) & (lane >= offset_lane) & (lane < dual_lane), -1.0, 0.0),
     )
-    spread[...] = jnp.where(target // depth == source % group, value, 0.0).astype(jnp.bfloat16)
-
-    pl.semaphore_wait(barrier, 2 * (group - 1))
+    spread[...] = jnp.where(target // depth == source % 8, value, 0.0).astype(jnp.bfloat16)
+
+    pl.semaphore_wait(barrier, len(partners))
 
     def spot_copy(pair, source=0, first=0, count=width, flight=None):
         target = z_shift_of(pair) - z_shift_of(source)
@@ -203,7 +205,6 @@
             device_id_type=MESH,
         )
 
-    line = (1, 2, 3)
     spot_direct = [spot_copy(pair) for pair in (3, 4, 1, 2)]
     spot_further = [
         spot_copy(5, 3),
@@ -228,16 +229,16 @@
         cell_copy(0, i).wait_recv()
         for j in line:
             cell_turn(j, i, False).start()
+    for pair in (1, 2):
+        spot_copy(pair).wait_recv()
+        passes[pair].start()
     for pair in (3, 4):
         spot_copy(pair).wait_recv()
     for step in spot_further:
         step.start()
-    for pair in (1, 2):
-        spot_copy(pair).wait_recv()
-    for pair in range(1, 5):
+    for pair in (3, 4):
         passes[pair].start()
-    for pair in range(5):
-        passes[pair].wait_recv()
+    passes[0].wait_recv()
 
     def further():
         for step in spot_further:
@@ -326,6 +327,8 @@
 
     def first_tiles(step, newest):
         chunk = 2 * step
+        spot_pass(chunk + 1).wait_recv()
+        spot_pass(chunk + 2).wait_recv()
         second = fill_near(chunk + 1, tile_b)
         absorb_near(chunk, tile_a, newest)
         third = fill_near(chunk + 2, tile_a)
@@ -338,24 +341,24 @@
     absorb_near(4, tile_a, newest)
     newest = fill_far(3, tile_a)
     absorb_far(4, tile_b, second)
-    second = fill_far(2, tile_b)
-    absorb_far(3, tile_a, newest)
-    newest = fill_far(1, tile_a)
-    absorb_far(2, tile_b, second)
     for pair in (5, 6, 7):
         passes[pair].wait_recv()
 
     def last_tiles(step, newest):
-        chunk = 5 + step
+        chunk = 7 - step
         second = fill_near(chunk, tile_b)
-        absorb_far(jnp.where(step == 0, 1, chunk - 1), tile_a, newest)
+        absorb_far(jnp.where(step == 0, 3, chunk + 1), tile_a, newest)
         third = fill_far(chunk, tile_a)
         absorb_near(chunk, tile_b, second)
         return third
 
     newest = lax.fori_loop(0, 3, last_tiles, newest)
+    second = fill_far(2, tile_b)
+    absorb_far(5, tile_a, newest)
+    newest = fill_far(1, tile_a)
+    absorb_far(2, tile_b, second)
     second = fill_far(0, tile_b)
-    absorb_far(7, tile_a, newest)
+    absorb_far(1, tile_a, newest)
     absorb_far(0, tile_b, second)
 
     sent()
@@ -378,19 +381,23 @@
             device_id_type=MESH,
         )
 
-    for slot in range(1, group):
+    for slot in range(group - 1, 0, -1):
         dual_copy(slot).start()
-    for slot in range(1, group):
+
+    def take_terms(part):
+        values = dual[8 * part:8 * part + 8, :]
+        high = values.astype(jnp.bfloat16).astype(jnp.float32)
+        middle = (values - high).astype(jnp.bfloat16).astype(jnp.float32)
+        low = values - high - middle
+        stacked = jnp.concatenate([high, middle, low, jnp.ones_like(low)], axis=0)
+        moved = dot_first(stacked.astype(jnp.bfloat16), spread[...]).astype(jnp.bfloat16)
+        for at in range(8):
+            own = slice((8 * part + at) * width, (8 * part + at + 1) * width)
+            spots[own, :] = spots[own, :] + moved[:, at * depth:(at + 1) * depth]
+
+    for slot in range(1, 8):
         dual_copy(slot).wait()
-    values = dual[...]
-    high = values.astype(jnp.bfloat16).astype(jnp.float32)
-    middle = (values - high).astype(jnp.bfloat16).astype(jnp.float32)
-    low = values - high - middle
-    stacked = jnp.concatenate([high, middle, low, jnp.ones_like(low)], axis=0).astype(jnp.bfloat16)
-    moved = dot_first(stacked, spread[...]).astype(jnp.bfloat16)
-    for slot in range(group):
-        at = slice(slot * width, (slot + 1) * width)
-        spots[at, :] = spots[at, :] + moved[:, slot * depth:(slot + 1) * depth]
+    take_terms(0)
 
     def part_2_copy(slot, target):
         return pltpu.make_async_remote_copy(
@@ -430,7 +437,11 @@
         close(chunk, finish_2)
         return third
 
-    newest = lax.fori_loop(0, chunks - 1, both, fill_2(0, chunks - 1, tile_a))
+    newest = fill_2(0, chunks - 1, tile_a)
+    for slot in range(8, group):
+        dual_copy(slot).wait()
+    take_terms(1)
+    newest = lax.fori_loop(0, chunks - 1, both, newest)
     second = fill_2(1, 0, tile_b)
     absorb(0, half_rows, tile_a, newest)
     absorb(0, half_rows, tile_b, second)
@@ -455,7 +466,7 @@
             pltpu.SemaphoreType.DMA((7,)),
             pltpu.VMEM((points, depth), jnp.bfloat16),
             pltpu.VMEM((points, depth), jnp.bfloat16),
-            pltpu.VMEM((4 * group, group * depth), jnp.bfloat16),
+            pltpu.VMEM((4 * 8, 8 * depth), jnp.bfloat16),
             pltpu.VMEM((far_rows, lanes), jnp.float32),
             pltpu.VMEM((far_rows, lanes), jnp.float32),
             pltpu.VMEM((chunks, 8, lanes), jnp.float32),

time: 57.7 us -> 53.6 us (0.929)
  Pallas kernels: 55 us -> 50.9 us
    pallas_call x1, Pallas kernels: 55 us -> 50.9 us  [local(): pl.pallas_call(kernel, out_shape=[jax.ShapeDtypeStruct((width,), jnp.floa...]
where the time goes in v4:
time: 53.6 us; the launch traced here: 53.4 us
  Pallas kernels  50.9 us (95%)
  local copies, waits for them, and re-layouts  1.86 us (3%)
  between operations  0.65 us (1%)
    pallas_call x1, Pallas kernels, local(): pl.pallas_call(kernel, out_shape=[jax.ShapeDtypeStruct((width,), jnp.floa...  50.9 us
    unnamed x6, local copies, waits for them, and re-layouts  1.86 us

profile of v4, /device:TPU:1, one launch (start us, length us, event | category | flops | bytes accessed | tf_op | source)
XLA Modules:
  0.0 53.4 jit_solution(14797575240514915167)
XLA Ops:
  0.6 50.9 %sweep.1 = (f32[192]{0:T(256)}, f32[192]{0:T(256)}) custom-call(bf16[64,192]{1,0:T(8,128)(2,1)} %spot_feat_in.1, bf16[34,192]{1,0:T(8,128)(2,1)} %spot_fac_in.1, f32[192]{0:T(256)} %spot_mass_in.1, bf16[64,192]{1,0:T(8,128)(2,1)} %cell_feat_in.1, bf16[34,192]{1,0:T(8,128)(2,1)} %cell_fac_in.1, f32[192]{0:T(256)} %cell_mass_in.1, f32[192]{0:T(256)} %cell_pot_in.1), custom_call_target="tpu_custom_call" | custom-call | tf_op jit(solution)/shard_map/sweep/pallas_call | solution.py:459
  51.6 0.0 copy-start.1
  51.6 0.7 %copy-done.1 = f32[192]{0:T(256)S(1)} copy-done((f32[192]{0:T(256)S(1)}, f32[192]{0:T(256)}, u32[]{:S(2)}) %copy-start.1) | copy-done | bytes 792
  52.2 0.0 copy-start
  52.2 0.6 %copy.11 = f32[192]{0:T(256)} copy(f32[192]{0:T(256)S(1)} %copy-done.1) | data formatting | bytes 1536
  52.8 0.1 copy-done
  52.9 0.6 %copy.12 = f32[192]{0:T(256)} copy(f32[192]{0:T(256)S(1)} %copy-done) | data formatting | bytes 1536
Async XLA Ops:
  51.6 0.7 %copy-start.1 = (f32[192]{0:T(256)S(1)}, f32[192]{0:T(256)}, u32[]{:S(2)}) copy-start(f32[192]{0:T(256)} %get-tuple-element.4) | copy-start | bytes 2308
  52.2 0.6 %copy-start = (f32[192]{0:T(256)S(1)}, f32[192]{0:T(256)}, u32[]{:S(2)}) copy-start(f32[192]{0:T(256)} %get-tuple-element.5) | copy-start | bytes 2308

commit v5 on v4

--- a/solution.py
+++ b/solution.py
@@ -14,11 +14,12 @@
 offset_lane = features + factors
 dual_lane = offset_lane + 3
 group = 16
-lanes = 384
+lanes = 768
+per_chunk = lanes // width
 chunks = group * width // lanes
 near_rows = 7 * width
 far_rows = 9 * width
-half_rows = group * width // 2
+near_part, far_part, even_part = near_rows // 4, far_rows // 4, group * width // 8
 part_rows = width // 2
 lowest = -1e30
 MESH = pl.DeviceIdType.MESH
@@ -271,14 +272,24 @@
             jnp.exp(scores - after[None]), axis=0
         )
 
+    def through(jobs, pending):
+        for job in jobs:
+            by_row, first, count, by_lane, chunk = job
+            tile = tile_a if pending is None else pending[3]
+            newest = fill(by_row, first, count, by_lane, chunk, tile)
+            if pending is not None:
+                absorb(*pending[:2], pending[2], pending[4])
+            pending = (chunk, count, tile, tile_b if tile is tile_a else tile_a, newest)
+        return pending
+
     def close(chunk, finish):
         top = jnp.max(highest[chunk], axis=0, keepdims=True)
         sums = jnp.sum(total[chunk] * jnp.exp(highest[chunk] - top), axis=0, keepdims=True)
         finish(chunk, top, sums)
 
-    def store_pair(out, slot, top, sums, first):
-        out[slot, 0:1, 0:width] = top[:, first:first + width]
-        out[slot, 1:2, 0:width] = sums[:, first:first + width]
+    def store_pair(out, slot, top, sums, at):
+        out[slot, 0:1, :] = top[:, at * width:(at + 1) * width]
+        out[slot, 1:2, :] = sums[:, at * width:(at + 1) * width]
 
     def combine(part):
         top = part[0, 0:1, 0:width]
@@ -300,66 +311,51 @@
         )
 
     def finish_1(chunk, top, sums):
-        store_pair(out_1, 2 * chunk + 1, top, sums, width)
-        if isinstance(chunk, int) and chunk == 0:
+        last = isinstance(chunk, int)
+        if last:
             store_pair(part_1, 0, top, sums, 0)
-            part_1_copy(1, along_q(0, 1)).start()
-        else:
-            store_pair(out_1, 2 * chunk, top, sums, 0)
-            back = (8 - z_shift(chunk)) % 8
-            part_1_copy(2 * chunk, along_q(back, 0)).start()
-            part_1_copy(2 * chunk + 1, along_q(back, 1)).start()
-
-    def fill_near(chunk, tile):
-        return fill(cells, 0, near_rows, spots, chunk, tile)
-
-    def fill_far(chunk, tile):
-        return fill(cells, near_rows, far_rows, spots, chunk, tile)
-
-    def absorb_near(chunk, tile, newest):
-        absorb(chunk, near_rows, tile, newest)
-
-    def absorb_far(chunk, tile, newest):
-        absorb(chunk, far_rows, tile, newest)
-        close(chunk, finish_1)
+        for at in range(last, per_chunk):
+            slot = per_chunk * chunk + at
+            store_pair(out_1, slot, top, sums, at)
+            back = (8 - z_shift(slot // 2)) % 8
+            part_1_copy(slot, along_q(back, at % 2)).start()
+
+    def near_jobs(chunk):
+        return [(cells, part * near_part, near_part, spots, chunk) for part in range(4)]
+
+    def far_jobs(chunk):
+        return [(cells, near_rows + part * far_part, far_part, spots, chunk) for part in range(4)]
+
+    def rest(pending):
+        return pending[0], pending[1], pending[2], pending[4]
 
     clear()
-
-    def first_tiles(step, newest):
-        chunk = 2 * step
-        spot_pass(chunk + 1).wait_recv()
-        spot_pass(chunk + 2).wait_recv()
-        second = fill_near(chunk + 1, tile_b)
-        absorb_near(chunk, tile_a, newest)
-        third = fill_near(chunk + 2, tile_a)
-        absorb_near(chunk + 1, tile_b, second)
-        return third
-
-    newest = lax.fori_loop(0, 2, first_tiles, fill_near(0, tile_a))
+    passes[1].wait_recv()
+    pending = through(near_jobs(0), None)
+    for pair in (2, 3):
+        passes[pair].wait_recv()
+    pending = through(near_jobs(1), pending)
     further()
-    second = fill_far(4, tile_b)
-    absorb_near(4, tile_a, newest)
-    newest = fill_far(3, tile_a)
-    absorb_far(4, tile_b, second)
+    passes[4].wait_recv()
+    pending = through(far_jobs(1), pending)
     for pair in (5, 6, 7):
         passes[pair].wait_recv()
 
     def last_tiles(step, newest):
-        chunk = 7 - step
-        second = fill_near(chunk, tile_b)
-        absorb_far(jnp.where(step == 0, 3, chunk + 1), tile_a, newest)
-        third = fill_far(chunk, tile_a)
-        absorb_near(chunk, tile_b, second)
-        return third
-
-    newest = lax.fori_loop(0, 3, last_tiles, newest)
-    second = fill_far(2, tile_b)
-    absorb_far(5, tile_a, newest)
-    newest = fill_far(1, tile_a)
-    absorb_far(2, tile_b, second)
-    second = fill_far(0, tile_b)
-    absorb_far(1, tile_a, newest)
-    absorb_far(0, tile_b, second)
+        chunk = 3 - step
+        before = jnp.where(step == 0, 1, chunk + 1)
+        held = (before, far_part, tile_b, tile_a, newest)
+        held = through(near_jobs(chunk)[:1], held)
+        close(before, finish_1)
+        held = through(near_jobs(chunk)[1:] + far_jobs(chunk), held)
+        return held[4]
+
+    newest = lax.fori_loop(0, 2, last_tiles, pending[4])
+    pending = through(far_jobs(0)[:1], (2, far_part, tile_b, tile_a, newest))
+    close(jnp.int32(2), finish_1)
+    pending = through(far_jobs(0)[1:], pending)
+    absorb(*rest(pending))
+    close(0, finish_1)
 
     sent()
     for slot in range(1, group):
@@ -414,37 +410,34 @@
         return along_p((4 - shift(i)) % 4, (4 - shift(j)) % 4)
 
     def finish_2(chunk, top, sums):
-        store_pair(out_2, 2 * chunk + 1, top, sums, width)
-        if isinstance(chunk, int) and chunk == 0:
+        last = isinstance(chunk, int)
+        if last:
             store_pair(part_2, 0, top, sums, 0)
-            part_2_copy(1, owner(1)).start()
-        else:
-            store_pair(out_2, 2 * chunk, top, sums, 0)
-            part_2_copy(2 * chunk, owner(2 * chunk)).start()
-            part_2_copy(2 * chunk + 1, owner(2 * chunk + 1)).start()
+        for at in range(last, per_chunk):
+            slot = per_chunk * chunk + at
+            store_pair(out_2, slot, top, sums, at)
+            part_2_copy(slot, owner(slot)).start()
+
+    def even_jobs(chunk):
+        return [(spots, part * even_part, even_part, cells, chunk) for part in range(8)]
 
     clear()
-
-    def fill_2(part, chunk, tile):
-        return fill(spots, part * half_rows, half_rows, cells, chunk, tile)
-
-    def both(step, newest):
-        chunk = chunks - 1 - step
-        second = fill_2(1, chunk, tile_b)
-        absorb(chunk, half_rows, tile_a, newest)
-        third = fill_2(0, chunk - 1, tile_a)
-        absorb(chunk, half_rows, tile_b, second)
-        close(chunk, finish_2)
-        return third
-
-    newest = fill_2(0, chunks - 1, tile_a)
+    top_chunk = chunks - 1
+    pending = through(even_jobs(top_chunk)[:4], None)
     for slot in range(8, group):
         dual_copy(slot).wait()
     take_terms(1)
-    newest = lax.fori_loop(0, chunks - 1, both, newest)
-    second = fill_2(1, 0, tile_b)
-    absorb(0, half_rows, tile_a, newest)
-    absorb(0, half_rows, tile_b, second)
+    pending = through(even_jobs(top_chunk)[4:], pending)
+
+    def next_chunk(step, newest):
+        chunk = chunks - 2 - step
+        held = (chunk + 1, even_part, tile_b, tile_a, newest)
+        held = through(even_jobs(chunk)[:1], held)
+        close(chunk + 1, finish_2)
+        return through(even_jobs(chunk)[1:], held)[4]
+
+    newest = lax.fori_loop(0, chunks - 1, next_chunk, pending[4])
+    absorb(0, even_part, tile_b, newest)
     close(0, finish_2)
     for slot in range(1, group):
         part_2_copy(slot, owner(slot)).wait()
@@ -467,8 +460,8 @@
             pltpu.VMEM((points, depth), jnp.bfloat16),
             pltpu.VMEM((points, depth), jnp.bfloat16),
             pltpu.VMEM((4 * 8, 8 * depth), jnp.bfloat16),
-            pltpu.VMEM((far_rows, lanes), jnp.float32),
-            pltpu.VMEM((far_rows, lanes), jnp.float32),
+            pltpu.VMEM((far_part, lanes), jnp.float32),
+            pltpu.VMEM((far_part, lanes), jnp.float32),
             pltpu.VMEM((chunks, 8, lanes), jnp.float32),
             pltpu.VMEM((chunks, 8, lanes), jnp.float32),
             pltpu.VMEM((group, 2, width), jnp.float32),

time: 53.6 us -> 50.5 us (0.942)
  Pallas kernels: 50.9 us -> 47.8 us
    pallas_call x1, Pallas kernels: 50.9 us -> 47.8 us  [local(): pl.pallas_call(kernel, out_shape=[jax.ShapeDtypeStruct((width,), jnp.floa...]
where the time goes in v5:
time: 50.5 us; the launch traced here: 50.4 us
  Pallas kernels  47.8 us (95%)
  local copies, waits for them, and re-layouts  1.86 us (4%)
  between operations  0.65 us (1%)
    pallas_call x1, Pallas kernels, local(): pl.pallas_call(kernel, out_shape=[jax.ShapeDtypeStruct((width,), jnp.floa...  47.8 us
    unnamed x6, local copies, waits for them, and re-layouts  1.86 us

profile of v5, /device:TPU:1, one launch (start us, length us, event | category | flops | bytes accessed | tf_op | source)
XLA Modules:
  0.0 50.4 jit_solution(8361836502909881106)
XLA Ops:
  0.6 47.8 %sweep.1 = (f32[192]{0:T(256)}, f32[192]{0:T(256)}) custom-call(bf16[64,192]{1,0:T(8,128)(2,1)} %spot_feat_in.1, bf16[34,192]{1,0:T(8,128)(2,1)} %spot_fac_in.1, f32[192]{0:T(256)} %spot_mass_in.1, bf16[64,192]{1,0:T(8,128)(2,1)} %cell_feat_in.1, bf16[34,192]{1,0:T(8,128)(2,1)} %cell_fac_in.1, f32[192]{0:T(256)} %cell_mass_in.1, f32[192]{0:T(256)} %cell_pot_in.1), custom_call_target="tpu_custom_call" | custom-call | tf_op jit(solution)/shard_map/sweep/pallas_call | solution.py:452
  48.5 0.0 copy-start.1
  48.5 0.7 %copy-done.1 = f32[192]{0:T(256)S(1)} copy-done((f32[192]{0:T(256)S(1)}, f32[192]{0:T(256)}, u32[]{:S(2)}) %copy-start.1) | copy-done | bytes 792
  49.2 0.0 copy-start
  49.2 0.6 %copy.11 = f32[192]{0:T(256)} copy(f32[192]{0:T(256)S(1)} %copy-done.1) | data formatting | bytes 1536
  49.7 0.1 copy-done
  49.8 0.6 %copy.12 = f32[192]{0:T(256)} copy(f32[192]{0:T(256)S(1)} %copy-done) | data formatting | bytes 1536
Async XLA Ops:
  48.5 0.7 %copy-start.1 = (f32[192]{0:T(256)S(1)}, f32[192]{0:T(256)}, u32[]{:S(2)}) copy-start(f32[192]{0:T(256)} %get-tuple-element.4) | copy-start | bytes 2308
  49.2 0.6 %copy-start = (f32[192]{0:T(256)S(1)}, f32[192]{0:T(256)}, u32[]{:S(2)}) copy-start(f32[192]{0:T(256)} %get-tuple-element.5) | copy-start | bytes 2308

commit v6 on v5

--- a/solution.py
+++ b/solution.py
@@ -63,8 +63,16 @@
     return jnp.sum(values * values, axis=0, keepdims=True) * (1.0 / (features * epsilon))
 
 
+def rem(value, by):
+    return value % by if isinstance(value, int) else lax.rem(value, jnp.int32(by))
+
+
+def div(value, by):
+    return value // by if isinstance(value, int) else lax.div(value, jnp.int32(by))
+
+
 def z_shift(pair):
-    return jnp.where(pair % 2 == 1, (pair + 1) // 2, (8 - pair // 2) % 8)
+    return jnp.where(rem(pair, 2) == 1, div(pair + 1, 2), rem(8 - div(pair, 2), 8))
 
 
 def z_shift_of(pair):
@@ -72,7 +80,7 @@
 
 
 def shift(place):
-    return place + (place // 2) * (5 - 2 * place)
+    return place + div(place, 2) * (5 - 2 * place)
 
 
 def slot_of(i, j):
@@ -82,14 +90,14 @@
 
 
 def lines_of(slot):
-    i = jnp.where(slot < 4, slot, jnp.where(slot < 7, 0, 1 + (slot + 2) % 3))
-    j = jnp.where(slot < 4, 0, jnp.where(slot < 7, slot - 3, 1 + (slot - 7) // 3))
+    i = jnp.where(slot < 4, slot, jnp.where(slot < 7, 0, 1 + rem(slot + 2, 3)))
+    j = jnp.where(slot < 4, 0, jnp.where(slot < 7, slot - 3, div(slot - 4, 3)))
     return i, j
 
 
 def kernel(
     spot_feat_in, spot_fac_in, spot_mass_in, cell_feat_in, cell_fac_in, cell_mass_in, cell_pot_in,
-    spot_out, cell_out,
+    out,
     spot_feat, spot_fac, spot_mass, cell_feat, cell_fac, cell_mass, cell_pot, input_sem,
     spots, cells, spread, tile_a, tile_b, highest, total,
     part_1, out_1, dual, part_2, out_2,
@@ -97,18 +105,27 @@
     part_1_send, part_1_recv, dual_send, dual_recv, part_2_send, part_2_recv,
 ):
     blk, grp = lax.axis_index("blk"), lax.axis_index("grp")
-    my_x, my_y = (blk // 4) * 2 + grp // 16, blk % 4
-    my_z, my_core = (grp % 16) // 2, grp % 2
-
-    def place(x, y, z, core):
-        return ((x // 2) * 4 + y, (x % 2) * 16 + z * 2 + core)
+    my_x, my_y = div(blk, 4) * 2 + div(grp, 16), rem(blk, 4)
+    my_z, my_core = div(rem(grp, 16), 2), rem(grp, 2)
+    same_x = grp - rem(grp, 16)
 
     def along_q(shift, other):
-        return place(my_x, my_y, (my_z + shift) % 8, (my_core + other) % 2)
+        return (blk, same_x + rem(my_z + shift, 8) * 2 + rem(my_core + other, 2))
 
     def along_p(dx, dy):
-        return place((my_x + dx) % 4, (my_y + dy) % 4, my_z, my_core)
-
+        x, y = rem(my_x + dx, 4), rem(my_y + dy, 4)
+        return (div(x, 2) * 4 + y, rem(x, 2) * 16 + rem(grp, 16))
+
+    barrier = pltpu.get_barrier_semaphore()
+    line = (1, 2, 3)
+    partners = (
+        [along_q(0, 1)]
+        + [along_q(z_shift_of(pair), 0) for pair in range(1, 5)]
+        + [along_p(shift(i), 0) for i in line]
+        + [along_p(0, shift(j)) for j in line]
+    )
+    for partner in partners:
+        pl.semaphore_signal(barrier, inc=1, device_id=partner, device_id_type=MESH)
     loads = [
         pltpu.make_async_copy(source, target, input_sem.at[at])
         for at, (source, target) in enumerate((
@@ -120,16 +137,6 @@
     for load in loads:
         load.start()
 
-    barrier = pltpu.get_barrier_semaphore()
-    line = (1, 2, 3)
-    partners = (
-        [along_q(0, 1)]
-        + [along_q(z_shift_of(pair), 0) for pair in range(1, 5)]
-        + [along_p(shift(i), 0) for i in line]
-        + [along_p(0, shift(j)) for j in line]
-    )
-    for partner in partners:
-        pl.semaphore_signal(barrier, inc=1, device_id=partner, device_id_type=MESH)
     for load in loads:
         load.wait()
 
@@ -149,17 +156,11 @@
     own_cells = jnp.where(lane_between(dual_lane, dual_lane + 3), 1.0, own_cells)
     cells[0:width, :] = own_cells.astype(jnp.bfloat16)
 
-    source = lax.broadcasted_iota(jnp.int32, spread.shape, 0)
-    target = lax.broadcasted_iota(jnp.int32, spread.shape, 1)
-    lane, kind = target % depth, source // 8
-    value = jnp.where(
-        lane == dual_lane + kind,
-        jnp.where(kind < 3, 1.0, 0.0),
-        jnp.where((kind == 3) & (lane >= offset_lane) & (lane < dual_lane), -1.0, 0.0),
-    )
-    spread[...] = jnp.where(target // depth == source % 8, value, 0.0).astype(jnp.bfloat16)
-
     pl.semaphore_wait(barrier, len(partners))
+
+    def clear():
+        highest[...] = jnp.full(highest.shape, lowest, jnp.float32)
+        total[...] = jnp.zeros(total.shape, jnp.float32)
 
     def spot_copy(pair, source=0, first=0, count=width, flight=None):
         target = z_shift_of(pair) - z_shift_of(source)
@@ -219,10 +220,21 @@
     ]
     passes = [spot_pass(pair) for pair in range(8)]
     passes[0].start()
-    for spot_step, cell_step in zip(spot_direct, ((0, 3), (1, 4), (2,), (5,))):
+    for spot_step, cell_step in zip(spot_direct, ((2, 5), (0, 3), (1,), (4,))):
         spot_step.start()
         for at in cell_step:
             cell_direct[at].start()
+    source = lax.broadcasted_iota(jnp.int32, spread.shape, 0)
+    target = lax.broadcasted_iota(jnp.int32, spread.shape, 1)
+    lane, kind = target % depth, source // 8
+    value = jnp.where(
+        lane == dual_lane + kind,
+        jnp.where(kind < 3, 1.0, 0.0),
+        jnp.where((kind == 3) & (lane >= offset_lane) & (lane < dual_lane), -1.0, 0.0),
+    )
+    spread[...] = jnp.where(target // depth == source % 8, value, 0.0).astype(jnp.bfloat16)
+
+    clear()
     for i in line:
         cell_copy(i, 0).wait_recv()
         for j in line:
@@ -253,10 +265,6 @@
         for step in spot_direct + spot_further + cell_direct + cell_turns + passes:
             step.wait_send()
 
-    def clear():
-        highest[...] = jnp.full(highest.shape, lowest, jnp.float32)
-        total[...] = jnp.zeros(total.shape, jnp.float32)
-
     def fill(by_row, first, count, by_lane, chunk, tile):
         right = by_lane[pl.ds(pl.multiple_of(chunk * lanes, lanes), lanes), :]
         scores = dot_last(by_row[pl.ds(first, count), :], right)
@@ -317,7 +325,7 @@
         for at in range(last, per_chunk):
             slot = per_chunk * chunk + at
             store_pair(out_1, slot, top, sums, at)
-            back = (8 - z_shift(slot // 2)) % 8
+            back = rem(8 - z_shift(div(slot, 2)), 8)
             part_1_copy(slot, along_q(back, at % 2)).start()
 
     def near_jobs(chunk):
@@ -329,7 +337,6 @@
     def rest(pending):
         return pending[0], pending[1], pending[2], pending[4]
 
-    clear()
     passes[1].wait_recv()
     pending = through(near_jobs(0), None)
     for pair in (2, 3):
@@ -364,7 +371,7 @@
     mass = spot_mass[...].reshape(1, width)
     log_count = math.log(256 * width)
     term = mass - log_sum + log_count
-    spot_out[...] = (epsilon * (term + norms(spot_feat[...]))).reshape(width)
+    out[0:1, :] = epsilon * (term + norms(spot_feat[...]))
     dual[0:1, :] = term
 
     def dual_copy(slot):
@@ -407,7 +414,7 @@
 
     def owner(slot):
         i, j = lines_of(slot)
-        return along_p((4 - shift(i)) % 4, (4 - shift(j)) % 4)
+        return along_p(4 - shift(i), 4 - shift(j))
 
     def finish_2(chunk, top, sums):
         last = isinstance(chunk, int)
@@ -443,17 +450,17 @@
         part_2_copy(slot, owner(slot)).wait()
     log_sum = combine(part_2)
     mass = cell_mass[...].reshape(1, width)
-    cell_out[...] = (epsilon * (mass - log_sum + norms(cell_feat[...]) + log_count)).reshape(width)
+    out[1:2, :] = epsilon * (mass - log_sum + norms(cell_feat[...]) + log_count)
 
 
 def local(*arguments):
     vmem = pl.BlockSpec(memory_space=pltpu.VMEM)
     points = group * width
-    return pl.pallas_call(
+    both = pl.pallas_call(
         kernel,
-        out_shape=[jax.ShapeDtypeStruct((width,), jnp.float32)] * 2,
+        out_shape=jax.ShapeDtypeStruct((2, width), jnp.float32),
         in_specs=[pl.BlockSpec(memory_space=pl.ANY)] * 7,
-        out_specs=[vmem] * 2,
+        out_specs=vmem,
         scratch_shapes=[pltpu.VMEM(value.shape, value.dtype) for value in arguments]
         + [
             pltpu.SemaphoreType.DMA((7,)),
@@ -477,6 +484,7 @@
         ),
         name="sweep",
     )(*arguments)
+    return both[0], both[1]
 
 
 def solution(mesh):

time: 50.5 us -> 49.8 us (0.986)
  local copies, waits for them, and re-layouts: 1.86 us -> 1.32 us
    unnamed x6 -> x0, local copies, waits for them, and re-layouts: 1.86 us -> none
    slice x0 -> x1, local copies, waits for them, and re-layouts: none -> 1.32 us  [local(): return (both[0], both[1])]
where the time goes in v6:
time: 49.8 us; the launch traced here: 49.6 us
  Pallas kernels  47.7 us (96%)
  local copies, waits for them, and re-layouts  1.32 us (3%)
  between operations  0.64 us (1%)
    pallas_call x1, Pallas kernels, local(): pl.pallas_call(kernel, out_shape=jax.ShapeDtypeStruct((2, width), jnp.flo...  47.7 us
    slice x1, local copies, waits for them, and re-layouts, local(): return (both[0], both[1])  1.32 us

profile of v6, /device:TPU:1, one launch (start us, length us, event | category | flops | bytes accessed | tf_op | source)
XLA Modules:
  0.0 49.6 jit_solution(15521784349434668206)
XLA Ops:
  0.6 47.7 %sweep.1 = f32[2,192]{1,0:T(2,128)} custom-call(bf16[64,192]{1,0:T(8,128)(2,1)} %spot_feat_in.1, bf16[34,192]{1,0:T(8,128)(2,1)} %spot_fac_in.1, f32[192]{0:T(256)} %spot_mass_in.1, bf16[64,192]{1,0:T(8,128)(2,1)} %cell_feat_in.1, bf16[34,192]{1,0:T(8,128)(2,1)} %cell_fac_in.1, f32[192]{0:T(256)} %cell_mass_in.1, f32[192]{0:T(256)} %cell_pot_in.1), custom_call_target="tpu_custom_call" | custom-call | tf_op jit(solution)/shard_map/sweep/pallas_call | solution.py:459
  48.3 1.3 %fusion = (f32[1,192]{1,0:T(1,128)}, f32[1,192]{1,0:T(1,128)}) fusion(f32[2,192]{1,0:T(2,128)} %sweep.1), kind=kLoop, calls=%fused_computation | loop fusion | bytes 3072 | tf_op jit(solution)/shard_map/slice | solution.py:487

commit v7 on v6

--- a/solution.py
+++ b/solution.py
@@ -19,7 +19,7 @@
 chunks = group * width // lanes
 near_rows = 7 * width
 far_rows = 9 * width
-near_part, far_part, even_part = near_rows // 4, far_rows // 4, group * width // 8
+near_part, far_part, even_part = near_rows // 6, far_rows // 6, group * width // 12
 part_rows = width // 2
 lowest = -1e30
 MESH = pl.DeviceIdType.MESH
@@ -329,10 +329,10 @@
             part_1_copy(slot, along_q(back, at % 2)).start()
 
     def near_jobs(chunk):
-        return [(cells, part * near_part, near_part, spots, chunk) for part in range(4)]
+        return [(cells, part * near_part, near_part, spots, chunk) for part in range(6)]
 
     def far_jobs(chunk):
-        return [(cells, near_rows + part * far_part, far_part, spots, chunk) for part in range(4)]
+        return [(cells, near_rows + part * far_part, far_part, spots, chunk) for part in range(6)]
 
     def rest(pending):
         return pending[0], pending[1], pending[2], pending[4]
@@ -426,15 +426,15 @@
             part_2_copy(slot, owner(slot)).start()
 
     def even_jobs(chunk):
-        return [(spots, part * even_part, even_part, cells, chunk) for part in range(8)]
+        return [(spots, part * even_part, even_part, cells, chunk) for part in range(12)]
 
     clear()
     top_chunk = chunks - 1
-    pending = through(even_jobs(top_chunk)[:4], None)
+    pending = through(even_jobs(top_chunk)[:6], None)
     for slot in range(8, group):
         dual_copy(slot).wait()
     take_terms(1)
-    pending = through(even_jobs(top_chunk)[4:], pending)
+    pending = through(even_jobs(top_chunk)[6:], pending)
 
     def next_chunk(step, newest):
         chunk = chunks - 2 - step

time: 49.8 us -> 49.7 us (level)
  no operation moved by 1% of the time
where the time goes in v7:
time: 49.7 us; the launch traced here: 49.6 us
  Pallas kernels  47.6 us (96%)
  local copies, waits for them, and re-layouts  1.32 us (3%)
  between operations  0.64 us (1%)
    pallas_call x1, Pallas kernels, local(): pl.pallas_call(kernel, out_shape=jax.ShapeDtypeStruct((2, width), jnp.flo...  47.6 us
    slice x1, local copies, waits for them, and re-layouts, local(): return (both[0], both[1])  1.32 us

profile of v7, /device:TPU:1, one launch (start us, length us, event | category | flops | bytes accessed | tf_op | source)
XLA Modules:
  0.0 49.6 jit_solution(16549009845564025505)
XLA Ops:
  0.6 47.6 %sweep.1 = f32[2,192]{1,0:T(2,128)} custom-call(bf16[64,192]{1,0:T(8,128)(2,1)} %spot_feat_in.1, bf16[34,192]{1,0:T(8,128)(2,1)} %spot_fac_in.1, f32[192]{0:T(256)} %spot_mass_in.1, bf16[64,192]{1,0:T(8,128)(2,1)} %cell_feat_in.1, bf16[34,192]{1,0:T(8,128)(2,1)} %cell_fac_in.1, f32[192]{0:T(256)} %cell_mass_in.1, f32[192]{0:T(256)} %cell_pot_in.1), custom_call_target="tpu_custom_call" | custom-call | tf_op jit(solution)/shard_map/sweep/pallas_call | solution.py:459
  48.2 1.3 %fusion = (f32[1,192]{1,0:T(1,128)}, f32[1,192]{1,0:T(1,128)}) fusion(f32[2,192]{1,0:T(2,128)} %sweep.1), kind=kLoop, calls=%fused_computation | loop fusion | bytes 3072 | tf_op jit(solution)/shard_map/slice | solution.py:487
